TPU v7x, 512 devices: a whole 4x4x16 slice. The times are simulated.
512 devices in a mesh: section: 8 (over x, core), expert: 16 (over z), dp: 4 (over y).
Axes of the slice: x: 4, y: 4, z: 16, core: 2. Of those that a mesh axis runs over, the one named last changes fastest.
Arguments:
- frames: bfloat16 [4, 128, 48, 1280], P(None, ('expert', 'dp')), may hold values from -6 to 6
- norm_gain: float32 [8, 1280], P('section'), may hold values from 0.1 to 1.9
- router: bfloat16 [8, 1280, 16], P('section'), may hold values from -0.15625 to 0.15625
- w_in: bfloat16 [8, 16, 1280, 256], P('section', 'expert'), may hold values from -0.15625 to 0.15625
- w_out: bfloat16 [8, 16, 256, 1280], P('section', 'expert'), may hold values from -0.375 to 0.375
- routing: int32 [8, 4, 128, 48, 1], P('section', None, ('expert', 'dp')), may hold values from 0 to 15; in each aligned block of 96 rows (0 to 95, 96 to 191, ..., all dimensions but the last counted through in order) at most 7 rows name the same one
- head_gain: float32 [1280], replicated, may hold values from 0.1 to 1.9
- head_weight: bfloat16 [1280, 8000], P(None, 'expert'), may hold values from -6 to 6
- frame_lengths: int32 [4, 128], P(None, ('expert', 'dp')), may hold values from 24 to 48
- labels: int32 [4, 128, 12], P(None, ('expert', 'dp')), may hold values from 1 to 7999
- label_lengths: int32 [4, 128], P(None, ('expert', 'dp')), may hold values from 1 to 12
Outputs:
- losses: float32 [8, 64], P('section', ('expert', 'dp'))
- head_grad: bfloat16 [1280, 8000], P(None, 'expert')
Inputs may be any that keep to these rules, and one draw needn't show every extreme that they name: `routing`: in each layer and micro-batch, within the frames of one device (aligned blocks of 96 frames), no expert is named by more than 7 frames.
All inputs are finite; a program needn't handle non-finite values.
Results may differ from a plain program's by a relative error of at most 0.015.
Values may be sent and summed in bfloat16 or wider, within the bound.
A program may use at most 64 MiB of HBM per device.

v0:
```python
import jax
import jax.numpy as jnp
from jax import lax
from jax.sharding import PartitionSpec as P

EPSILON = 1e-06
LOG_ZERO = -1e30


def shifted(value, axis, by):
    count = lax.axis_size(axis)
    pairs = [(i, i + by) for i in range(count) if 0 <= i + by < count]
    return lax.ppermute(value, axis, pairs)


def from_root(block, axis, owner):
    block = jnp.where(lax.axis_index(axis) == owner, block, jnp.zeros_like(block))
    return lax.psum(block, axis)


def rms_scale(values, scaling):
    values = values.astype(jnp.float32)
    return values * lax.rsqrt(jnp.mean(values * values, axis=-1, keepdims=True) + EPSILON) * scaling


def extend_labels(label_rows):
    blanks = jnp.zeros_like(label_rows)
    paired = jnp.stack([blanks, label_rows], axis=-1).reshape(
        label_rows.shape[:-1] + (2 * label_rows.shape[-1],)
    )
    return jnp.concatenate([paired, jnp.zeros(label_rows.shape[:-1] + (1,), jnp.int32)], axis=-1)


def ctc_single(emission, ext_labels, frame_count, label_count):
    state_count = ext_labels.shape[0]
    position = jnp.arange(state_count, dtype=jnp.int32)
    earlier = jnp.concatenate([jnp.full((2,), -1, jnp.int32), ext_labels[:-2]])
    skippable = (ext_labels != 0) & (ext_labels != earlier) & (position >= 2)
    lowest = jnp.full((state_count,), LOG_ZERO, emission.dtype)
    initial = jnp.where(position < 2, emission[0], lowest)

    def advance(forward_log, inputs):
        emit_row, time_step = inputs
        one_back = jnp.concatenate([lowest[:1], forward_log[:-1]])
        two_back = jnp.where(skippable, jnp.concatenate([lowest[:2], forward_log[:-2]]), lowest)
        moved = jnp.logaddexp(jnp.logaddexp(forward_log, one_back), two_back) + emit_row
        return (jnp.where(time_step < frame_count, moved, forward_log), None)

    time_steps = jnp.arange(1, emission.shape[0], dtype=jnp.int32)
    final_log, _ = lax.scan(advance, initial, (emission[1:], time_steps))
    last_state = 2 * label_count
    end_state = jnp.sum(jnp.where(position == last_state, final_log, 0.0))
    near_state = jnp.sum(jnp.where(position == last_state - 1, final_log, 0.0))
    return -jnp.logaddexp(end_state, near_state)


def ctc_terms(emission, ext_labels, frame_counts, label_counts):

    def summed_loss(values):
        losses = jax.vmap(ctc_single)(values, ext_labels, frame_counts, label_counts)
        return (jnp.sum(losses), losses)

    summed, pullback, losses = jax.vjp(summed_loss, emission, has_aux=True)
    occupancy = pullback(jnp.ones_like(summed))[0]
    return (losses, occupancy)


def per_device(
    frames,
    norm_gain,
    router,
    w_in,
    w_out,
    routing,
    head_gain,
    head_weight,
    frame_lengths,
    labels,
    label_lengths,
):
    sections = lax.axis_size("section")
    section_id = lax.axis_index("section")
    group_size = lax.axis_size("expert")
    member = lax.axis_index("expert")
    micro, utt_dev, frame_count, width = frames.shape
    tokens = utt_dev * frame_count
    local_experts = w_in.shape[1]
    experts = local_experts * group_size
    capacity = (tokens * 9 + 8 * experts - 1) // (8 * experts)
    layer_gain = norm_gain[0]
    router_w = router[0]
    weight_in = w_in[0]
    weight_out = w_out[0]
    section_routes = routing[0, :, :, :, 0].reshape(micro, tokens)
    micro_inputs = frames.reshape(micro, tokens, width)

    def expert_block(piece):
        slot_count = piece.shape[1]
        grouped = piece.reshape(group_size, local_experts, slot_count, width)
        hidden = jnp.einsum(
            "glcd,ldh->glch", grouped, weight_in, preferred_element_type=jnp.float32
        )
        active = (hidden * jax.nn.sigmoid(hidden)).astype(jnp.bfloat16)
        result = jnp.einsum(
            "glch,lhd->glcd", active, weight_out, preferred_element_type=jnp.float32
        )
        return result.astype(jnp.bfloat16).reshape(group_size * local_experts, slot_count, width)

    def section_layer(current, expert_ids):
        normed = rms_scale(current, layer_gain).astype(jnp.bfloat16)
        logits = jnp.dot(normed, router_w, preferred_element_type=jnp.float32)
        one_hot = (expert_ids[:, None] == jnp.arange(experts, dtype=jnp.int32)[None, :]).astype(
            jnp.int32
        )
        slot_rank = jnp.sum((jnp.cumsum(one_hot, axis=0) - 1) * one_hot, axis=1)
        target_slot = expert_ids * capacity + slot_rank
        gate_value = jax.nn.sigmoid(jnp.sum(jnp.where(one_hot > 0, logits, 0.0), axis=1))
        outgoing = jnp.zeros((experts * capacity, width), jnp.bfloat16).at[target_slot].set(normed)
        outgoing = outgoing.reshape(experts, capacity, width)
        processed = expert_block(
            lax.all_to_all(outgoing, "expert", split_axis=0, concat_axis=0, tiled=True)
        )
        returned = lax.all_to_all(
            processed, "expert", split_axis=0, concat_axis=0, tiled=True
        ).reshape(experts * capacity, width)
        mixed = returned[target_slot].astype(jnp.float32)
        return (current.astype(jnp.float32) + gate_value[:, None] * mixed).astype(jnp.bfloat16)

    def run_tick(tick_index, incoming, collected):
        micro_id = jnp.clip(tick_index - section_id, 0, micro - 1)
        fresh = lax.dynamic_index_in_dim(
            micro_inputs, jnp.clip(tick_index, 0, micro - 1), 0, keepdims=False
        )
        current = jnp.where(section_id == 0, fresh, incoming)
        expert_ids = lax.dynamic_index_in_dim(section_routes, micro_id, 0, keepdims=False)
        produced = section_layer(current, expert_ids)
        usable = (
            (section_id == sections - 1)
            & (tick_index >= section_id)
            & (tick_index - section_id < micro)
        )
        updated = lax.dynamic_update_index_in_dim(collected, produced, micro_id, 0)
        return (produced, jnp.where(usable, updated, collected))

    def loop_body(tick_index, carry):
        produced, collected = carry
        incoming = shifted(produced, "section", 1)
        return run_tick(tick_index, incoming, collected)

    collected = jnp.zeros((micro, tokens, width), jnp.bfloat16)
    produced, collected = run_tick(0, micro_inputs[0], collected)
    produced, collected = lax.fori_loop(1, micro + sections - 1, loop_body, (produced, collected))
    pair_count = micro * utt_dev
    per_section = pair_count // sections
    first_pair = section_id * per_section
    finished = from_root(collected, "section", sections - 1)
    pair_rows = finished.reshape(pair_count, frame_count, width)
    my_rows = lax.dynamic_slice_in_dim(pair_rows, first_pair, per_section, 0)
    my_labels = lax.dynamic_slice_in_dim(
        labels.reshape(pair_count, labels.shape[2]), first_pair, per_section, 0
    )
    length_pairs = jnp.stack(
        [frame_lengths.reshape(pair_count), label_lengths.reshape(pair_count)], axis=1
    )
    my_counts = lax.dynamic_slice_in_dim(length_pairs, first_pair, per_section, 0)
    head_normed = rms_scale(my_rows, head_gain).astype(jnp.bfloat16)
    rows_all, labels_all, counts_all = (
        lax.all_gather(head_normed, "expert", axis=0, tiled=True),
        lax.all_gather(my_labels, "expert", axis=0, tiled=True),
        lax.all_gather(my_counts, "expert", axis=0, tiled=True),
    )
    shard = head_weight.shape[1]
    utterance_count = rows_all.shape[0]
    row_count = utterance_count * frame_count
    flat_rows = rows_all.reshape(row_count, width)
    logits = jnp.dot(flat_rows, head_weight, preferred_element_type=jnp.float32)
    local_peak = jnp.max(logits, axis=1)
    highest = lax.pmax(local_peak, "expert")
    denominator = lax.psum(jnp.sum(jnp.exp(logits - highest[:, None]), axis=1), "expert")
    log_total = highest + jnp.log(denominator)
    logprob = (logits - log_total[:, None]).reshape(utterance_count, frame_count, shard)
    ext_all = extend_labels(labels_all)
    columns = member * shard + jnp.arange(shard, dtype=jnp.int32)
    selector = (ext_all[:, :, None] == columns[None, None, :]).astype(jnp.float32)
    emission_part = jnp.einsum("btv,bsv->bts", logprob, selector, precision=lax.Precision.HIGHEST)
    emission = lax.psum_scatter(emission_part, "expert", scatter_dimension=0, tiled=True)
    losses, own_occupancy = ctc_terms(
        emission, extend_labels(my_labels), my_counts[:, 0], my_counts[:, 1]
    )
    occupancy = lax.all_gather(own_occupancy, "expert", axis=0, tiled=True)
    scattered = jnp.einsum("bts,bsv->btv", occupancy, selector, precision=lax.Precision.HIGHEST)
    grad_logits = (scattered - jnp.exp(logprob) * jnp.sum(occupancy, axis=2, keepdims=True)).astype(
        jnp.bfloat16
    )
    grad_flat = grad_logits.reshape(row_count, shard)
    partial_grad = lax.dot_general(
        flat_rows, grad_flat, (((0,), (0,)), ((), ())), preferred_element_type=jnp.float32
    )
    head_grad = lax.psum(partial_grad, ("section", "dp")).astype(jnp.bfloat16)
    return (losses.reshape(per_section, 1), head_grad)


def solution(mesh):
    placed = (
        P(None, ("expert", "dp"), None, None),
        P("section", None),
        P("section", None, None),
        P("section", "expert", None, None),
        P("section", "expert", None, None),
        P("section", None, ("expert", "dp"), None, None),
        P(),
        P(None, "expert"),
        P(None, ("expert", "dp")),
        P(None, ("expert", "dp"), None),
        P(None, ("expert", "dp")),
    )
    return jax.shard_map(
        per_device,
        mesh=mesh,
        in_specs=placed,
        out_specs=(P("section", ("expert", "dp")), P(None, "expert")),
        check_vma=False,
    )
```

profile of v0, /device:TPU:1, one launch (start us, length us, event | category | flops | bytes accessed | tf_op | source)
XLA Modules:
  0.0 1294.8 jit_solution(1041347805522192852)
XLA Ops:
  13.8 30.8 %all_to_all.36 = bf16[16,7,1280]{2,1,0:T(8,128)(2,1)S(1)} all-to-all(bf16[16,7,1280]{2,1,0:T(8,128)(2,1)S(1)} %reshape.530), channel_id=1, replica_groups=mesh['section'=8,'expert'=16,'dp'=4] {'expert'}, dimensions={0} | all-to-all | bytes 573440 | tf_op jit(solution)/shard_map/all_to_all | solution.py:121
  60.2 13.7 %all-to-all-done.3 = bf16[16,7,1280]{2,1,0:T(8,128)(2,1)S(1)} async-done(((bf16[16,7,1280]{2,1,0:T(8,128)(2,1)}), bf16[16,7,1280]{2,1,0:T(8,128)(2,1)S(1)}, u32[]{:S(2)}, u32[]{:S(2)}) %all-to-all-start.3) | async-done | bytes 286752 | tf_op jit(solution)/shard_map/all_to_all | solution.py:123
  77.1 625.1 %while.54 = (s32[]{:T(128)}, bf16[96,1280]{1,0:T(8,128)(2,1)S(1)}, bf16[4,96,1280]{2,1,0:T(8,128)(2,1)S(1)}, pred[]{:T(512)}, bf16[4,96,1280]{2,1,0:T(8,128)(2,1...) while((s32[]{:T(128)}, bf16[96,1280]{1,0:T(8,128)(2,1)S(1)}, ...), condition=%wide.region_11.12_spmd, body=%wide.region_5.11_spmd.sunk | while | flops 153395888 | bytes 9464925 | solution.py:152
  92.2 24.5 %all_to_all.37 = bf16[16,7,1280]{2,1,0:T(8,128)(2,1)S(1)} all-to-all(bf16[16,7,1280]{2,1,0:T(8,128)(2,1)S(1)} %reshape.611), channel_id=1, replica_groups=mesh['section'=8,'expert'=16,'dp'=4] {'expert'}, dimensions={0} | all-to-all | bytes 573440 | tf_op jit(solution)/shard_map/while/body/eval_jaxpr/all_to_all | solution.py:121
  125.4 15.2 %all-to-all-done.1 = bf16[16,7,1280]{2,1,0:T(8,128)(2,1)S(1)} async-done(((bf16[16,7,1280]{2,1,0:T(8,128)(2,1)}), bf16[16,7,1280]{2,1,0:T(8,128)(2,1)S(1)}, u32[]{:S(2)}, u32[]{:S(2)}) %all-to-all-start.1) | async-done | bytes 286752 | tf_op jit(solution)/shard_map/while/body/eval_jaxpr/all_to_all | solution.py:123
  158.8 22.4 %all_to_all.37 = bf16[16,7,1280]{2,1,0:T(8,128)(2,1)S(1)} all-to-all(bf16[16,7,1280]{2,1,0:T(8,128)(2,1)S(1)} %reshape.611), channel_id=1, replica_groups=mesh['section'=8,'expert'=16,'dp'=4] {'expert'}, dimensions={0} | all-to-all | bytes 573440 | tf_op jit(solution)/shard_map/while/body/eval_jaxpr/all_to_all | solution.py:121
  189.8 18.4 %all-to-all-done.1 = bf16[16,7,1280]{2,1,0:T(8,128)(2,1)S(1)} async-done(((bf16[16,7,1280]{2,1,0:T(8,128)(2,1)}), bf16[16,7,1280]{2,1,0:T(8,128)(2,1)S(1)}, u32[]{:S(2)}, u32[]{:S(2)}) %all-to-all-start.1) | async-done | bytes 286752 | tf_op jit(solution)/shard_map/while/body/eval_jaxpr/all_to_all | solution.py:123
  224.5 19.1 %all_to_all.37 = bf16[16,7,1280]{2,1,0:T(8,128)(2,1)S(1)} all-to-all(bf16[16,7,1280]{2,1,0:T(8,128)(2,1)S(1)} %reshape.611), channel_id=1, replica_groups=mesh['section'=8,'expert'=16,'dp'=4] {'expert'}, dimensions={0} | all-to-all | bytes 573440 | tf_op jit(solution)/shard_map/while/body/eval_jaxpr/all_to_all | solution.py:121
  252.8 16.6 %all-to-all-done.1 = bf16[16,7,1280]{2,1,0:T(8,128)(2,1)S(1)} async-done(((bf16[16,7,1280]{2,1,0:T(8,128)(2,1)}), bf16[16,7,1280]{2,1,0:T(8,128)(2,1)S(1)}, u32[]{:S(2)}, u32[]{:S(2)}) %all-to-all-start.1) | async-done | bytes 286752 | tf_op jit(solution)/shard_map/while/body/eval_jaxpr/all_to_all | solution.py:123
  286.7 19.0 %all_to_all.37 = bf16[16,7,1280]{2,1,0:T(8,128)(2,1)S(1)} all-to-all(bf16[16,7,1280]{2,1,0:T(8,128)(2,1)S(1)} %reshape.611), channel_id=1, replica_groups=mesh['section'=8,'expert'=16,'dp'=4] {'expert'}, dimensions={0} | all-to-all | bytes 573440 | tf_op jit(solution)/shard_map/while/body/eval_jaxpr/all_to_all | solution.py:121
  329.6 13.6 %collective-permute-start = (bf16[96,1280]{1,0:T(8,128)(2,1)S(1)}, bf16[96,1280]{1,0:T(8,128)(2,1)S(1)}, u32[]{:S(2)}, u32[]{:S(2)}) collective-permute-start(bf16[96,1280]{1,0:T(8,128)(2,1)S(1)} %get-tuple-element.920), channel_id=1, source_target_pairs={{0,64},{64,128},{128,192},{192,256},{256,320},{320,384},{384,448},... | collective-permute-start | bytes 737288 | tf_op jit(solution)/shard_map/while/body/eval_jaxpr/ppermute | solution.py:13
  348.8 19.1 %all_to_all.37 = bf16[16,7,1280]{2,1,0:T(8,128)(2,1)S(1)} all-to-all(bf16[16,7,1280]{2,1,0:T(8,128)(2,1)S(1)} %reshape.611), channel_id=1, replica_groups=mesh['section'=8,'expert'=16,'dp'=4] {'expert'}, dimensions={0} | all-to-all | bytes 573440 | tf_op jit(solution)/shard_map/while/body/eval_jaxpr/all_to_all | solution.py:121
  392.0 13.5 %collective-permute-start = (bf16[96,1280]{1,0:T(8,128)(2,1)S(1)}, bf16[96,1280]{1,0:T(8,128)(2,1)S(1)}, u32[]{:S(2)}, u32[]{:S(2)}) collective-permute-start(bf16[96,1280]{1,0:T(8,128)(2,1)S(1)} %get-tuple-element.920), channel_id=1, source_target_pairs={{0,64},{64,128},{128,192},{192,256},{256,320},{320,384},{384,448},... | collective-permute-start | bytes 737288 | tf_op jit(solution)/shard_map/while/body/eval_jaxpr/ppermute | solution.py:13
  411.0 19.0 %all_to_all.37 = bf16[16,7,1280]{2,1,0:T(8,128)(2,1)S(1)} all-to-all(bf16[16,7,1280]{2,1,0:T(8,128)(2,1)S(1)} %reshape.611), channel_id=1, replica_groups=mesh['section'=8,'expert'=16,'dp'=4] {'expert'}, dimensions={0} | all-to-all | bytes 573440 | tf_op jit(solution)/shard_map/while/body/eval_jaxpr/all_to_all | solution.py:121
  453.9 13.6 %collective-permute-start = (bf16[96,1280]{1,0:T(8,128)(2,1)S(1)}, bf16[96,1280]{1,0:T(8,128)(2,1)S(1)}, u32[]{:S(2)}, u32[]{:S(2)}) collective-permute-start(bf16[96,1280]{1,0:T(8,128)(2,1)S(1)} %get-tuple-element.920), channel_id=1, source_target_pairs={{0,64},{64,128},{128,192},{192,256},{256,320},{320,384},{384,448},... | collective-permute-start | bytes 737288 | tf_op jit(solution)/shard_map/while/body/eval_jaxpr/ppermute | solution.py:13
  473.1 19.0 %all_to_all.37 = bf16[16,7,1280]{2,1,0:T(8,128)(2,1)S(1)} all-to-all(bf16[16,7,1280]{2,1,0:T(8,128)(2,1)S(1)} %reshape.611), channel_id=1, replica_groups=mesh['section'=8,'expert'=16,'dp'=4] {'expert'}, dimensions={0} | all-to-all | bytes 573440 | tf_op jit(solution)/shard_map/while/body/eval_jaxpr/all_to_all | solution.py:121
  516.1 13.5 %collective-permute-start = (bf16[96,1280]{1,0:T(8,128)(2,1)S(1)}, bf16[96,1280]{1,0:T(8,128)(2,1)S(1)}, u32[]{:S(2)}, u32[]{:S(2)}) collective-permute-start(bf16[96,1280]{1,0:T(8,128)(2,1)S(1)} %get-tuple-element.920), channel_id=1, source_target_pairs={{0,64},{64,128},{128,192},{192,256},{256,320},{320,384},{384,448},... | collective-permute-start | bytes 737288 | tf_op jit(solution)/shard_map/while/body/eval_jaxpr/ppermute | solution.py:13
  535.1 19.0 %all_to_all.37 = bf16[16,7,1280]{2,1,0:T(8,128)(2,1)S(1)} all-to-all(bf16[16,7,1280]{2,1,0:T(8,128)(2,1)S(1)} %reshape.611), channel_id=1, replica_groups=mesh['section'=8,'expert'=16,'dp'=4] {'expert'}, dimensions={0} | all-to-all | bytes 573440 | tf_op jit(solution)/shard_map/while/body/eval_jaxpr/all_to_all | solution.py:121
  563.7 13.3 %all-to-all-done.1 = bf16[16,7,1280]{2,1,0:T(8,128)(2,1)S(1)} async-done(((bf16[16,7,1280]{2,1,0:T(8,128)(2,1)}), bf16[16,7,1280]{2,1,0:T(8,128)(2,1)S(1)}, u32[]{:S(2)}, u32[]{:S(2)}) %all-to-all-start.1) | async-done | bytes 286752 | tf_op jit(solution)/shard_map/while/body/eval_jaxpr/all_to_all | solution.py:123
  578.1 13.6 %collective-permute-start = (bf16[96,1280]{1,0:T(8,128)(2,1)S(1)}, bf16[96,1280]{1,0:T(8,128)(2,1)S(1)}, u32[]{:S(2)}, u32[]{:S(2)}) collective-permute-start(bf16[96,1280]{1,0:T(8,128)(2,1)S(1)} %get-tuple-element.920), channel_id=1, source_target_pairs={{0,64},{64,128},{128,192},{192,256},{256,320},{320,384},{384,448},... | collective-permute-start | bytes 737288 | tf_op jit(solution)/shard_map/while/body/eval_jaxpr/ppermute | solution.py:13
  597.2 19.0 %all_to_all.37 = bf16[16,7,1280]{2,1,0:T(8,128)(2,1)S(1)} all-to-all(bf16[16,7,1280]{2,1,0:T(8,128)(2,1)S(1)} %reshape.611), channel_id=1, replica_groups=mesh['section'=8,'expert'=16,'dp'=4] {'expert'}, dimensions={0} | all-to-all | bytes 573440 | tf_op jit(solution)/shard_map/while/body/eval_jaxpr/all_to_all | solution.py:121
  640.3 13.5 %collective-permute-start = (bf16[96,1280]{1,0:T(8,128)(2,1)S(1)}, bf16[96,1280]{1,0:T(8,128)(2,1)S(1)}, u32[]{:S(2)}, u32[]{:S(2)}) collective-permute-start(bf16[96,1280]{1,0:T(8,128)(2,1)S(1)} %get-tuple-element.920), channel_id=1, source_target_pairs={{0,64},{64,128},{128,192},{192,256},{256,320},{320,384},{384,448},... | collective-permute-start | bytes 737288 | tf_op jit(solution)/shard_map/while/body/eval_jaxpr/ppermute | solution.py:13
  659.3 19.0 %all_to_all.37 = bf16[16,7,1280]{2,1,0:T(8,128)(2,1)S(1)} all-to-all(bf16[16,7,1280]{2,1,0:T(8,128)(2,1)S(1)} %reshape.611), channel_id=1, replica_groups=mesh['section'=8,'expert'=16,'dp'=4] {'expert'}, dimensions={0} | all-to-all | bytes 573440 | tf_op jit(solution)/shard_map/while/body/eval_jaxpr/all_to_all | solution.py:121
  703.4 79.8 %all-reduce.12.cloned.1.call-done = bf16[8,48,1280]{2,1,0:T(8,128)(2,1)} async-done(((bf16[8,48,1280]{2,1,0:T(8,128)(2,1)}), bf16[8,48,1280]{2,1,0:T(8,128)(2,1)}) %all-reduce.12.cloned.1.call-update) | async-done | bytes 983056 | tf_op jit(solution)/shard_map/psum | solution.py:18
  787.1 22.7 %all-gather = s32[16,1,12]{2,1,0:T(1,128)S(1)} all-gather(s32[1,1,12]{2,1,0:T(1,128)S(1)} %get-tuple-element.681), channel_id=1, replica_groups=mesh['section'=8,'expert'=16,'dp'=4] {'expert'}, dimensions={0}, use_global_device_ids=true | all-gather | bytes 816 | tf_op jit(solution)/shard_map/all_gather | solution.py:169
  810.5 41.2 %all-gather.3.cloned.1.call-done = bf16[16,48,1280]{2,1,0:T(8,128)(2,1)} async-done(((bf16[1,48,1280]{2,1,0:T(8,128)(2,1)}), bf16[16,48,1280]{2,1,0:T(8,128)(2,1)}) %all-gather.3.cloned.1.call-update) | async-done | bytes 1966096 | tf_op jit(solution)/shard_map/all_gather | solution.py:168
  854.5 21.4 %pmax.7 = f32[768]{0:T(1024)S(1)} all-reduce(f32[768]{0:T(1024)S(1)} %get-tuple-element.684), channel_id=1, replica_groups=mesh['section'=8,'expert'=16,'dp'=4] {'expert'}, use_global_device_ids=true, to_apply=%region_15.16 | all-reduce | flops 768 | bytes 6144 | tf_op jit(solution)/shard_map/pmax | solution.py:178
  876.2 20.5 %psum.22 = f32[768]{0:T(1024)S(1)} all-reduce(f32[768]{0:T(1024)S(1)} %exponential_reduce_fusion), channel_id=1, replica_groups=mesh['section'=8,'expert'=16,'dp'=4] {'expert'}, use_global_device_ids=true, to_apply=%region_17.18 | all-reduce | flops 768 | bytes 6144 | tf_op jit(solution)/shard_map/psum | solution.py:179
  902.4 76.2 %reduce-scatter.2.cloned.1.call-done = f32[1,48,25]{1,2,0:T(8,128)} async-done(((f32[16,48,25]{1,2,0:T(8,128)}), f32[1,48,25]{1,2,0:T(8,128)}) %reduce-scatter.2.cloned.1.call-update) | async-done | bytes 4816 | tf_op jit(solution)/shard_map/reduce_scatter | solution.py:186
  980.4 98.8 %while.55 = (s32[]{:T(128)}, f32[1,25]{1,0:T(1,128)S(1)}, f32[47,1,25]{2,1,0:T(1,128)S(1)}, f32[47,1,25]{2,1,0:T(1,128)S(1)}, f32[47,1,25]{2,1,0:T(1,128)S(1)}, ...) while((s32[]{:T(128)}, f32[1,25]{1,0:T(1,128)S(1)}, ...), condition=%wide.region_20.21_spmd, body=%wide.region_19.20_spmd.sunk | while | flops 1303 | bytes 5673 | solution.py:50
  1096.4 22.6 %all_gather.11 = f32[16,48,25]{1,2,0:T(8,128)S(1)} all-gather(f32[1,48,25]{1,2,0:T(8,128)S(1)} %copy.60), channel_id=1, replica_groups=mesh['section'=8,'expert'=16,'dp'=4] {'expert'}, dimensions={0}, use_global_device_ids=true | all-gather | bytes 81600 | tf_op jit(solution)/shard_map/all_gather | solution.py:190
  1123.4 163.7 %all-reduce.13 = bf16[1280,500]{0,1:T(8,128)(2,1)} all-reduce(f32[1280,500]{0,1:T(8,128)} %convolution_bitcast_fusion.1), channel_id=1, replica_groups=mesh['section'=8,'expert'=16,'dp'=4] {'section','dp'}, use_global_device_ids=true, to_apply=%region_26.27 | all-reduce | flops 640000 | bytes 3840000 | tf_op jit(solution)/shard_map/psum | solution.py:199
  (845 shorter events, 383.4 us)
Async XLA Ops:
  7.2 844.5 %copy-start = (bf16[1280,500]{0,1:T(8,128)(2,1)S(1)}, bf16[1280,500]{0,1:T(8,128)(2,1)}, u32[]{:S(2)}) copy-start(bf16[1280,500]{0,1:T(8,128)(2,1)} %param.24) | copy-start | bytes 3840004
  44.5 15.4 %copy-start.2 = (bf16[1,1280,16]{1,2,0:T(8,128)(2,1)S(1)}, bf16[1,1280,16]{1,2,0:T(8,128)(2,1)}, u32[]{:S(2)}) copy-start(bf16[1,1280,16]{1,2,0:T(8,128)(2,1)} %param.19) | copy-start | bytes 122884
  47.2 26.7 %all-to-all-start.3 = ((bf16[16,7,1280]{2,1,0:T(8,128)(2,1)}), bf16[16,7,1280]{2,1,0:T(8,128)(2,1)S(1)}, u32[]{:S(2)}, u32[]{:S(2)}) async-start(bf16[16,7,1280]{2,1,0:T(8,128)(2,1)} %copy.51), calls=%async_computation.3 | async-start | bytes 655360 | tf_op jit(solution)/shard_map/all_to_all | solution.py:123
  58.8 724.4 %all-reduce.12.cloned.1.call-start = ((), (), s32[]{:S(2)}) async-start(), calls=%async_computation.5 | async-start | bytes 1966080 | tf_op jit(solution)/shard_map/psum | solution.py:18
  74.8 2.3 copy-start.1
  77.1 12.6 collective-permute-start
  119.4 21.2 %all-to-all-start.1 = ((bf16[16,7,1280]{2,1,0:T(8,128)(2,1)}), bf16[16,7,1280]{2,1,0:T(8,128)(2,1)S(1)}, u32[]{:S(2)}, u32[]{:S(2)}) async-start(bf16[16,7,1280]{2,1,0:T(8,128)(2,1)} %copy.89), calls=%async_computation.1 | async-start | bytes 655360 | tf_op jit(solution)/shard_map/while/body/eval_jaxpr/all_to_all | solution.py:123
  141.8 14.6 %collective-permute-start = (bf16[96,1280]{1,0:T(8,128)(2,1)S(1)}, bf16[96,1280]{1,0:T(8,128)(2,1)S(1)}, u32[]{:S(2)}, u32[]{:S(2)}) collective-permute-start(bf16[96,1280]{1,0:T(8,128)(2,1)S(1)} %get-tuple-element.920), channel_id=1, source_target_pairs={{0,64},{64,128},{128,192},{192,256},{256,320},{320,384},{384,448},... | collective-permute-start | bytes 737288 | tf_op jit(solution)/shard_map/while/body/eval_jaxpr/ppermute | solution.py:13
  184.0 24.2 %all-to-all-start.1 = ((bf16[16,7,1280]{2,1,0:T(8,128)(2,1)}), bf16[16,7,1280]{2,1,0:T(8,128)(2,1)S(1)}, u32[]{:S(2)}, u32[]{:S(2)}) async-start(bf16[16,7,1280]{2,1,0:T(8,128)(2,1)} %copy.89), calls=%async_computation.1 | async-start | bytes 655360 | tf_op jit(solution)/shard_map/while/body/eval_jaxpr/all_to_all | solution.py:123
  209.3 12.7 collective-permute-start
  246.3 23.1 %all-to-all-start.1 = ((bf16[16,7,1280]{2,1,0:T(8,128)(2,1)}), bf16[16,7,1280]{2,1,0:T(8,128)(2,1)S(1)}, u32[]{:S(2)}, u32[]{:S(2)}) async-start(bf16[16,7,1280]{2,1,0:T(8,128)(2,1)} %copy.89), calls=%async_computation.1 | async-start | bytes 655360 | tf_op jit(solution)/shard_map/while/body/eval_jaxpr/all_to_all | solution.py:123
  270.5 13.8 %collective-permute-start = (bf16[96,1280]{1,0:T(8,128)(2,1)S(1)}, bf16[96,1280]{1,0:T(8,128)(2,1)S(1)}, u32[]{:S(2)}, u32[]{:S(2)}) collective-permute-start(bf16[96,1280]{1,0:T(8,128)(2,1)S(1)} %get-tuple-element.920), channel_id=1, source_target_pairs={{0,64},{64,128},{128,192},{192,256},{256,320},{320,384},{384,448},... | collective-permute-start | bytes 737288 | tf_op jit(solution)/shard_map/while/body/eval_jaxpr/ppermute | solution.py:13
  308.4 20.1 %all-to-all-start.1 = ((bf16[16,7,1280]{2,1,0:T(8,128)(2,1)}), bf16[16,7,1280]{2,1,0:T(8,128)(2,1)S(1)}, u32[]{:S(2)}, u32[]{:S(2)}) async-start(bf16[16,7,1280]{2,1,0:T(8,128)(2,1)} %copy.89), calls=%async_computation.1 | async-start | bytes 655360 | tf_op jit(solution)/shard_map/while/body/eval_jaxpr/all_to_all | solution.py:123
  329.6 16.8 %collective-permute-start = (bf16[96,1280]{1,0:T(8,128)(2,1)S(1)}, bf16[96,1280]{1,0:T(8,128)(2,1)S(1)}, u32[]{:S(2)}, u32[]{:S(2)}) collective-permute-start(bf16[96,1280]{1,0:T(8,128)(2,1)S(1)} %get-tuple-element.920), channel_id=1, source_target_pairs={{0,64},{64,128},{128,192},{192,256},{256,320},{320,384},{384,448},... | collective-permute-start | bytes 737288 | tf_op jit(solution)/shard_map/while/body/eval_jaxpr/ppermute | solution.py:13
  370.6 20.2 %all-to-all-start.1 = ((bf16[16,7,1280]{2,1,0:T(8,128)(2,1)}), bf16[16,7,1280]{2,1,0:T(8,128)(2,1)S(1)}, u32[]{:S(2)}, u32[]{:S(2)}) async-start(bf16[16,7,1280]{2,1,0:T(8,128)(2,1)} %copy.89), calls=%async_computation.1 | async-start | bytes 655360 | tf_op jit(solution)/shard_map/while/body/eval_jaxpr/all_to_all | solution.py:123
  392.0 16.6 %collective-permute-start = (bf16[96,1280]{1,0:T(8,128)(2,1)S(1)}, bf16[96,1280]{1,0:T(8,128)(2,1)S(1)}, u32[]{:S(2)}, u32[]{:S(2)}) collective-permute-start(bf16[96,1280]{1,0:T(8,128)(2,1)S(1)} %get-tuple-element.920), channel_id=1, source_target_pairs={{0,64},{64,128},{128,192},{192,256},{256,320},{320,384},{384,448},... | collective-permute-start | bytes 737288 | tf_op jit(solution)/shard_map/while/body/eval_jaxpr/ppermute | solution.py:13
  432.7 20.1 %all-to-all-start.1 = ((bf16[16,7,1280]{2,1,0:T(8,128)(2,1)}), bf16[16,7,1280]{2,1,0:T(8,128)(2,1)S(1)}, u32[]{:S(2)}, u32[]{:S(2)}) async-start(bf16[16,7,1280]{2,1,0:T(8,128)(2,1)} %copy.89), calls=%async_computation.1 | async-start | bytes 655360 | tf_op jit(solution)/shard_map/while/body/eval_jaxpr/all_to_all | solution.py:123
  453.9 16.7 %collective-permute-start = (bf16[96,1280]{1,0:T(8,128)(2,1)S(1)}, bf16[96,1280]{1,0:T(8,128)(2,1)S(1)}, u32[]{:S(2)}, u32[]{:S(2)}) collective-permute-start(bf16[96,1280]{1,0:T(8,128)(2,1)S(1)} %get-tuple-element.920), channel_id=1, source_target_pairs={{0,64},{64,128},{128,192},{192,256},{256,320},{320,384},{384,448},... | collective-permute-start | bytes 737288 | tf_op jit(solution)/shard_map/while/body/eval_jaxpr/ppermute | solution.py:13
  494.8 20.2 %all-to-all-start.1 = ((bf16[16,7,1280]{2,1,0:T(8,128)(2,1)}), bf16[16,7,1280]{2,1,0:T(8,128)(2,1)S(1)}, u32[]{:S(2)}, u32[]{:S(2)}) async-start(bf16[16,7,1280]{2,1,0:T(8,128)(2,1)} %copy.89), calls=%async_computation.1 | async-start | bytes 655360 | tf_op jit(solution)/shard_map/while/body/eval_jaxpr/all_to_all | solution.py:123
  516.1 16.6 %collective-permute-start = (bf16[96,1280]{1,0:T(8,128)(2,1)S(1)}, bf16[96,1280]{1,0:T(8,128)(2,1)S(1)}, u32[]{:S(2)}, u32[]{:S(2)}) collective-permute-start(bf16[96,1280]{1,0:T(8,128)(2,1)S(1)} %get-tuple-element.920), channel_id=1, source_target_pairs={{0,64},{64,128},{128,192},{192,256},{256,320},{320,384},{384,448},... | collective-permute-start | bytes 737288 | tf_op jit(solution)/shard_map/while/body/eval_jaxpr/ppermute | solution.py:13
  556.9 20.1 %all-to-all-start.1 = ((bf16[16,7,1280]{2,1,0:T(8,128)(2,1)}), bf16[16,7,1280]{2,1,0:T(8,128)(2,1)S(1)}, u32[]{:S(2)}, u32[]{:S(2)}) async-start(bf16[16,7,1280]{2,1,0:T(8,128)(2,1)} %copy.89), calls=%async_computation.1 | async-start | bytes 655360 | tf_op jit(solution)/shard_map/while/body/eval_jaxpr/all_to_all | solution.py:123
  578.1 16.7 %collective-permute-start = (bf16[96,1280]{1,0:T(8,128)(2,1)S(1)}, bf16[96,1280]{1,0:T(8,128)(2,1)S(1)}, u32[]{:S(2)}, u32[]{:S(2)}) collective-permute-start(bf16[96,1280]{1,0:T(8,128)(2,1)S(1)} %get-tuple-element.920), channel_id=1, source_target_pairs={{0,64},{64,128},{128,192},{192,256},{256,320},{320,384},{384,448},... | collective-permute-start | bytes 737288 | tf_op jit(solution)/shard_map/while/body/eval_jaxpr/ppermute | solution.py:13
  618.9 20.2 %all-to-all-start.1 = ((bf16[16,7,1280]{2,1,0:T(8,128)(2,1)}), bf16[16,7,1280]{2,1,0:T(8,128)(2,1)S(1)}, u32[]{:S(2)}, u32[]{:S(2)}) async-start(bf16[16,7,1280]{2,1,0:T(8,128)(2,1)} %copy.89), calls=%async_computation.1 | async-start | bytes 655360 | tf_op jit(solution)/shard_map/while/body/eval_jaxpr/all_to_all | solution.py:123
  640.3 16.6 %collective-permute-start = (bf16[96,1280]{1,0:T(8,128)(2,1)S(1)}, bf16[96,1280]{1,0:T(8,128)(2,1)S(1)}, u32[]{:S(2)}, u32[]{:S(2)}) collective-permute-start(bf16[96,1280]{1,0:T(8,128)(2,1)S(1)} %get-tuple-element.920), channel_id=1, source_target_pairs={{0,64},{64,128},{128,192},{192,256},{256,320},{320,384},{384,448},... | collective-permute-start | bytes 737288 | tf_op jit(solution)/shard_map/while/body/eval_jaxpr/ppermute | solution.py:13
  681.0 20.1 %all-to-all-start.1 = ((bf16[16,7,1280]{2,1,0:T(8,128)(2,1)}), bf16[16,7,1280]{2,1,0:T(8,128)(2,1)S(1)}, u32[]{:S(2)}, u32[]{:S(2)}) async-start(bf16[16,7,1280]{2,1,0:T(8,128)(2,1)} %copy.89), calls=%async_computation.1 | async-start | bytes 655360 | tf_op jit(solution)/shard_map/while/body/eval_jaxpr/all_to_all | solution.py:123
  702.3 82.0 %copy-start.3 = (f32[1280]{0:T(1024)S(1)}, f32[1280]{0:T(1024)}, u32[]{:S(2)}) copy-start(f32[1280]{0:T(1024)} %param.23) | copy-start | bytes 15364
  702.3 83.7 %copy-start.4 = (s32[4,2]{0,1:T(2,128)S(1)}, s32[4,2]{0,1:T(2,128)}, u32[]{:S(2)}) copy-start(s32[4,2]{0,1:T(2,128)} %param.25) | copy-start | bytes 100
  702.3 83.9 %copy-start.5 = (s32[4,2]{0,1:T(2,128)S(1)}, s32[4,2]{0,1:T(2,128)}, u32[]{:S(2)}) copy-start(s32[4,2]{0,1:T(2,128)} %param.27) | copy-start | bytes 100
  703.3 148.4 %all-gather.3.cloned.1.call-start = ((), (), s32[]{:S(2)}) async-start(), calls=%async_computation.6 | async-start | bytes 2088960 | tf_op jit(solution)/shard_map/all_gather | solution.py:168
  786.0 192.7 %reduce-scatter.2.cloned.1.call-start = ((), (), s32[]{:S(2)}) async-start(), calls=%async_computation.7 | async-start | bytes 278528 | tf_op jit(solution)/shard_map/reduce_scatter | solution.py:186
  1119.1 1.5 copy-start.6
Sparse Core Ops, SparseCore 0:
  703.5 79.7 all-reduce.11
  786.1 65.5 all-gather.2
  901.6 76.9 reduce-scatter.1
where the time goes:
time: 1300 us; the launch traced here: 1290 us
  blocking collectives  481 us (37%)
  waiting for transfers between devices  381 us (29%)
  starting transfers between devices  198 us (15%)
  local copies, waits for them, and re-layouts  65.4 us (5%)
  loops' own time  62 us (5%)
  other arithmetic  53.9 us (4%)
  matrix products  31.6 us (2%)
  between operations  22.4 us (2%)
    all_to_all x11, blocking collectives, section_layer(): lax.all_to_all(outgoing, 'expert', split_axis=0, concat_axis=0, tiled=True)  230 us
    psum x1, blocking collectives, per_device(): head_grad = lax.psum(partial_grad, ('section', 'dp')).astype(jnp.bfloat16)  164 us
    all_to_all x11, waiting for transfers between devices, section_layer(): lax.all_to_all(processed, 'expert', split_axis=0, concat_axis=0, tiled=True)  156 us
    ppermute x10, starting transfers between devices, shifted(): return lax.ppermute(value, axis, pairs)  122 us
    psum x1, waiting for transfers between devices, from_root(): return lax.psum(block, axis)  79.8 us
    reduce_scatter x1, waiting for transfers between devices, per_device(): lax.psum_scatter(emission_part, 'expert', scatter_dimension=0, tiled=True)  76.2 us
    all_to_all x11, starting transfers between devices, section_layer(): lax.all_to_all(processed, 'expert', split_axis=0, concat_axis=0, tiled=True)  75.4 us
    another operation x2, loops' own time, ctc_single(): final_log, _ = lax.scan(advance, initial, (emission[1:], time_steps))  60.3 us
  transfers between devices with their start and end apart: 24, of which 24 were waited for; matrix products, arithmetic and copies ran while one was open for 1% of the time, Pallas kernels for 0%

commit v1 on v0

v1 whole, which is shorter than its diff:
```python
import functools

import jax
import jax.numpy as jnp
from jax import lax
from jax.experimental import pallas as pl
from jax.experimental.pallas import tpu as pltpu
from jax.sharding import PartitionSpec as P

EPSILON = 1e-06
LOG_ZERO = -1e30
MESH = pl.DeviceIdType.MESH
F32, BF16 = jnp.float32, jnp.bfloat16
D, HALF, EFF, LAYERS, RING, TOK, FRAMES = 1280, 640, 256, 8, 16, 96, 48
PIECES = 8
CHUNKS = LAYERS * PIECES
IN_ROWS, OUT_ROWS = D // PIECES, EFF // PIECES
SHARD, WIDE = 500, 512
HIGHEST = lax.Precision.HIGHEST
VMEM = pltpu.VMEM
DMA = pltpu.SemaphoreType.DMA
VMEM_LIMIT = 56 * 1024 * 1024


def coords():
    s, z, y = lax.axis_index("section"), lax.axis_index("expert"), lax.axis_index("dp")
    return s, s // 2, lax.rem(s, 2), z, y


def loop(low, high, body):
    def step(i, carry):
        body(i)
        return carry

    lax.fori_loop(low, high, step, 0)


def remote(src, dst, send, recv, device):
    return pltpu.make_async_remote_copy(
        src_ref=src, dst_ref=dst, send_sem=send, recv_sem=recv, device_id=device, device_id_type=MESH
    )


def dot(a, b, dims=((1,), (0,)), precision=None):
    return lax.dot_general(a, b, (dims, ((), ())), precision=precision, preferred_element_type=F32)


def rms(x, gain):
    return (x * lax.rsqrt(jnp.mean(x * x, axis=-1, keepdims=True) + EPSILON) * gain).astype(BF16)


def moe_kernel(
    x0, w_in, w_out, router, aux, head_gain, hn_out,
    win, wout, routers, auxes, state, give, take, answer, back, stage_in, stage_out, passed, landed,
    got_in, got_out, on_in, on_out, copy_in, copy_out, have_in, have_out,
    lay_send, stage_send, stage_got, small_send, small_got, give_send, take_got, answer_send, back_got, hn_send, hn_got,
):
    s, x, c, z, y = coords()
    me = 4 * x + y
    home_x, home_y = z // 4, lax.rem(z, 4)
    above, below = lax.rem(z + 1, RING), lax.rem(z + RING - 1, RING)
    barrier = pltpu.get_barrier_semaphore()

    def greet(i):
        p = lax.rem(4 * s + y + i, 32)
        pl.semaphore_signal(barrier, inc=1, device_id=(p // 4, z, lax.rem(p, 4)), device_id_type=MESH)

    loop(1, 32, greet)
    pl.semaphore_signal(barrier, inc=1, device_id=(s, above, y), device_id_type=MESH)
    pl.semaphore_signal(barrier, inc=1, device_id=(s, below, y), device_id_type=MESH)
    pl.semaphore_wait(barrier, 33)

    def in_rows(j):
        return pl.ds(pl.multiple_of(j * IN_ROWS, 32), IN_ROWS)

    def out_rows(j):
        return pl.ds(pl.multiple_of(j * OUT_ROWS, 32), OUT_ROWS)

    def share(layer, i, src_in, src_out):
        j = y + 4 * i
        k = layer * PIECES + j
        target = (2 * home_x + 1, z, home_y)
        return (
            remote(src_in, win.at[layer, in_rows(j)], lay_send.at[2 * c, i], got_in.at[k], target),
            remote(src_out, wout.at[layer, out_rows(j)], lay_send.at[2 * c + 1, i], got_out.at[k], target),
        )

    def staged(i):
        j = y + 4 * i
        target = (s + 1, z, y)
        return (
            remote(w_in.at[in_rows(j)], stage_in.at[i], stage_send.at[0, i], stage_got.at[0, i], target),
            remote(w_out.at[out_rows(j)], stage_out.at[i], stage_send.at[1, i], stage_got.at[1, i], target),
        )

    def small(to_x):
        target = (2 * to_x, z, y)
        return (
            remote(aux, auxes.at[s], small_send.at[0, to_x], small_got.at[0, s], target),
            remote(router, routers.at[s], small_send.at[1, to_x], small_got.at[1, s], target),
        )

    def each(copies, act):
        for copy in copies:
            act(copy)

    start, sent, got = (lambda d: d.start()), (lambda d: d.wait_send()), (lambda d: d.wait_recv())

    @pl.when((c == 0) & (x == 0))
    def _():
        for i in range(2):
            each(share(0, i, w_in.at[in_rows(y + 4 * i)], w_out.at[out_rows(y + 4 * i)]), start)

    @pl.when((c == 0) & (x > 0))
    def _():
        for i in range(2):
            each(staged(i), start)

    for gap in range(1, 4):
        each(small(lax.rem(x + gap, 4)), start)

    own_small = (
        pltpu.make_async_copy(aux, auxes.at[s], small_got.at[0, s]),
        pltpu.make_async_copy(router, routers.at[s], small_got.at[1, s]),
    )

    @pl.when(c == 1)
    def _():
        each(small(x), start)

    @pl.when(c == 0)
    def _():
        each(own_small, start)

    @pl.when(c == 1)
    def _():
        at_home = (x == home_x) & (y == home_y)
        up, down = lax.rem(z + RING - me, RING), lax.rem(me + RING - z, RING)

        def distribute(layer, slot, pick):
            for i in range(2):
                j = y + 4 * i
                src_in, src_out = pick(i)

                @pl.when(at_home)
                def _():
                    k = layer * PIECES + j
                    pltpu.make_async_copy(src_in, win.at[layer, in_rows(j)], got_in.at[k]).start()
                    pltpu.make_async_copy(src_out, wout.at[layer, out_rows(j)], got_out.at[k]).start()

                @pl.when(jnp.logical_not(at_home))
                def _():
                    each(carried(layer, slot, i, src_in, src_out), start)

        def carried(layer, slot, i, src_in, src_out):
            j = y + 4 * i
            k = layer * PIECES + j
            target = (2 * home_x + 1, z, home_y)
            return (
                remote(src_in, win.at[layer, in_rows(j)], lay_send.at[2 * slot, i], got_in.at[k], target),
                remote(src_out, wout.at[layer, out_rows(j)], lay_send.at[2 * slot + 1, i], got_out.at[k], target),
            )

        def from_stage(i):
            return stage_in.at[i], stage_out.at[i]

        def from_own(i):
            return w_in.at[in_rows(y + 4 * i)], w_out.at[out_rows(y + 4 * i)]

        def rise(k):
            layer, j = k // PIECES, lax.rem(k, PIECES)
            ref = win.at[layer, in_rows(j)]
            return remote(ref, ref, on_in.at[k], got_in.at[k], (s, above, y))

        def sink(k):
            layer, j = k // PIECES, lax.rem(k, PIECES)
            ref = wout.at[layer, out_rows(j)]
            return remote(ref, ref, on_out.at[k], got_out.at[k], (s, below, y))

        def hand_in(layer):
            return remote(win.at[layer], win.at[layer], copy_in.at[layer], have_in.at[layer], (s - 1, z, y))

        def hand_out(layer):
            return remote(wout.at[layer], wout.at[layer], copy_out.at[layer], have_out.at[layer], (s - 1, z, y))

        def tick(t):
            @pl.when((x > 0) & (t == 16 * x - 8))
            def _():
                for i in range(2):
                    each(staged(i), got)
                distribute(2 * x, 0, from_stage)

            @pl.when(t == 16 * x)
            def _():
                distribute(2 * x + 1, 1, from_own)

            ku, kd = t - up, t - down

            @pl.when((ku >= 0) & (ku < CHUNKS))
            def _():
                rise(ku).wait_recv()

                @pl.when(up < RING - 1)
                def _():
                    rise(ku).start()

                @pl.when(lax.rem(ku, PIECES) == PIECES - 1)
                def _():
                    hand_in(ku // PIECES).start()

            @pl.when((kd >= 0) & (kd < CHUNKS))
            def _():
                sink(kd).wait_recv()

                @pl.when(down < RING - 1)
                def _():
                    sink(kd).start()

                @pl.when(lax.rem(kd, PIECES) == PIECES - 1)
                def _():
                    hand_out(kd // PIECES).start()

        loop(0, CHUNKS + RING - 1, tick)

        @pl.when(jnp.logical_not(at_home))
        def _():
            for i in range(2):
                @pl.when(x > 0)
                def _():
                    each(carried(2 * x, 0, i, *from_stage(i)), sent)

                each(carried(2 * x + 1, 1, i, *from_own(i)), sent)

        @pl.when(up < RING - 1)
        def _():
            loop(0, CHUNKS, lambda k: rise(k).wait_send())

        @pl.when(down < RING - 1)
        def _():
            loop(0, CHUNKS, lambda k: sink(k).wait_send())

        loop(0, LAYERS, lambda layer: hand_in(layer).wait_send())
        loop(0, LAYERS, lambda layer: hand_out(layer).wait_send())
        each(small(x), sent)

    @pl.when(c == 0)
    def _():
        state[...] = x0[...]

        def smalls(layer):
            pltpu.make_async_copy(aux, auxes.at[layer], small_got.at[0, layer]).wait()
            pltpu.make_async_copy(router, routers.at[layer], small_got.at[1, layer]).wait()

        loop(0, LAYERS, smalls)

        def chip(p):
            return (2 * (p // 4), z, lax.rem(p, 4))

        def out_to(p):
            return remote(give.at[p], take.at[me], give_send.at[p], take_got.at[me], chip(p))

        def in_from(p):
            return remote(give.at[p], take.at[p], give_send.at[p], take_got.at[p], chip(p))

        def back_to(p):
            return remote(answer.at[p], back.at[me], answer_send.at[p], back_got.at[me], chip(p))

        def back_from(p):
            return remote(answer.at[p], back.at[p], answer_send.at[p], back_got.at[p], chip(p))

        def others(act):
            loop(1, RING, lambda i: act(lax.rem(me + i, RING)))

        def layer_step(layer):
            xf = state[...].astype(F32)
            normed = rms(xf, auxes[layer, 0:1, :])
            which = lax.broadcasted_iota(jnp.int32, (8, 128), 0) == 1 + x
            spots = jnp.sum(jnp.where(which, auxes[layer, :, 0:128], 0.0), axis=0, keepdims=True)
            pick = (lax.broadcasted_iota(jnp.int32, (128, 128), 0).astype(F32) == spots)[:, :TOK]
            pick = pick.astype(F32).astype(BF16)
            left = dot(pick, normed[:, :HALF]).reshape(RING, 8, HALF)
            right = dot(pick, normed[:, HALF:]).reshape(RING, 8, HALF)
            give[...] = jnp.concatenate([left, right], axis=1).astype(BF16)
            others(lambda p: out_to(p).start())
            take[me] = give[me]

            columns = jnp.transpose(jnp.broadcast_to(spots, (128, 128)))[:TOK, :].astype(jnp.int32)
            lane = lax.broadcasted_iota(jnp.int32, (TOK, 128), 1)
            logits = dot(normed, routers[layer], ((1,), (1,)))
            mine = (lane[:, :RING] == (columns[:, :RING] >> 3)).astype(F32)
            gate = jax.nn.sigmoid(jnp.sum(mine * logits, axis=1, keepdims=True))
            place = columns + ((columns >> 3) << 3)
            spread = [(lane + 128 * h == place + 8 * b).astype(F32).astype(BF16) for b in range(2) for h in range(2)]
            put_left = jnp.concatenate(spread[:2], axis=1)
            put_right = jnp.concatenate(spread[2:], axis=1)

            pltpu.make_async_copy(win.at[layer], win.at[layer], have_in.at[layer]).wait()
            others(lambda p: in_from(p).wait_recv())
            rows = take[...].reshape(RING * 16, HALF)
            first = dot(rows, win[layer, 0:HALF, :]).reshape(RING, 16, EFF)
            second = dot(rows, win[layer, HALF:D, :]).reshape(RING, 16, EFF)
            hidden = (first[:, 0:8] + second[:, 8:16]).reshape(128, EFF)
            active = (hidden * jax.nn.sigmoid(hidden)).astype(BF16)
            pltpu.make_async_copy(wout.at[layer], wout.at[layer], have_out.at[layer]).wait()
            result = dot(active, wout[layer]).reshape(RING, 8, D)
            answer[...] = jnp.concatenate([result[:, :, :HALF], result[:, :, HALF:]], axis=1).astype(BF16)
            others(lambda p: back_to(p).start())
            back[me] = answer[me]
            others(lambda p: out_to(p).wait_send())
            others(lambda p: back_from(p).wait_recv())
            returned = back[...].reshape(RING * 16, HALF)
            mixed = jnp.concatenate([dot(put_left, returned), dot(put_right, returned)], axis=1)
            state[...] = (xf + gate * mixed).astype(BF16)
            others(lambda p: back_to(p).wait_send())

        loop(0, LAYERS, layer_step)
        hn = rms(state[...].astype(F32), head_gain[...])
        for h in range(2):
            hn_out[h] = hn[:FRAMES, HALF * h : HALF * (h + 1)]
            passed[h] = hn[FRAMES:, HALF * h : HALF * (h + 1)]
        remote(passed, landed, hn_send, hn_got, (s + 1, z, y)).start()

        @pl.when(x == 0)
        def _():
            for i in range(2):
                each(share(0, i, w_in.at[in_rows(y + 4 * i)], w_out.at[out_rows(y + 4 * i)]), sent)

        @pl.when(x > 0)
        def _():
            for i in range(2):
                each(staged(i), sent)

        remote(passed, landed, hn_send, hn_got, (s + 1, z, y)).wait_send()

    @pl.when(c == 1)
    def _():
        remote(passed, landed, hn_send, hn_got, (s, z, y)).wait_recv()
        hn_out[...] = landed[...]

    for gap in range(1, 4):
        each(small(lax.rem(x + gap, 4)), sent)


def run_moe(x0, w_in, w_out, router, aux, head_gain):
    anywhere, local = pl.BlockSpec(memory_space=pl.ANY), pl.BlockSpec(memory_space=VMEM)
    return pl.pallas_call(
        moe_kernel,
        out_shape=jax.ShapeDtypeStruct((2, FRAMES, HALF), BF16),
        in_specs=[local, anywhere, anywhere, local, local, local],
        out_specs=local,
        scratch_shapes=[
            VMEM((LAYERS, D, EFF), BF16),
            VMEM((LAYERS, EFF, D), BF16),
            VMEM((LAYERS, 16, D), BF16),
            VMEM((LAYERS, 8, D), F32),
            VMEM((TOK, D), BF16),
            VMEM((RING, 16, HALF), BF16),
            VMEM((RING, 16, HALF), BF16),
            VMEM((RING, 16, HALF), BF16),
            VMEM((RING, 16, HALF), BF16),
            VMEM((2, IN_ROWS, EFF), BF16),
            VMEM((2, OUT_ROWS, D), BF16),
            VMEM((2, FRAMES, HALF), BF16),
            VMEM((2, FRAMES, HALF), BF16),
            DMA((CHUNKS,)), DMA((CHUNKS,)), DMA((CHUNKS,)), DMA((CHUNKS,)),
            DMA((LAYERS,)), DMA((LAYERS,)), DMA((LAYERS,)), DMA((LAYERS,)),
            DMA((4, 2)), DMA((2, 2)), DMA((2, 2)), DMA((2, 4)), DMA((2, LAYERS)),
            DMA((RING,)), DMA((RING,)), DMA((RING,)), DMA((RING,)),
            DMA, DMA,
        ],
        compiler_params=pltpu.CompilerParams(
            collective_id=0, has_side_effects=True, vmem_limit_bytes=VMEM_LIMIT
        ),
    )(x0, w_in, w_out, router, aux, head_gain)


def flip(block):
    rows = block.shape[0]
    if rows < 128:
        block = jnp.concatenate([block, jnp.zeros((128 - rows, 128), F32)], axis=0)
    return jnp.transpose(block)


def pack(columns):
    turned = flip(columns)
    return turned[0:8] + pltpu.roll(turned[8:16], 64, 1)


def lanes(rows):
    return lax.broadcasted_iota(jnp.int32, (rows, 128), 1)


def triple(a, b, c):
    top = jnp.maximum(jnp.maximum(a, b), c)
    return top + jnp.log(jnp.exp(a - top) + jnp.exp(b - top) + jnp.exp(c - top))


def head_kernel(
    hn, weight, names, meta, loss_out, grad_out,
    rows_all, names_all, logits, stats, stats_all, emit, ahead, behind, notes, notes_all, grads, partial,
    half_out, half_in, pieces, pieces_all, total, totals,
    up_send, up_got, down_send, down_got, name_send, name_got, stat_send, stat_got, note_send, note_got,
    half_send, half_got, piece_send, piece_got, total_send, total_got, last_send, last_got,
):
    s, x, c, z, y = coords()
    me = 4 * x + y
    pair = (s + 1 - 2 * c, z, y)
    above, below = lax.rem(z + 1, RING), lax.rem(z + RING - 1, RING)
    barrier = pltpu.get_barrier_semaphore()

    def chip(p):
        return (2 * (p // 4) + c, z, lax.rem(p, 4))

    def greet(i):
        pl.semaphore_signal(barrier, inc=1, device_id=(s, lax.rem(z + i, RING), y), device_id_type=MESH)
        pl.semaphore_signal(barrier, inc=1, device_id=chip(lax.rem(me + i, RING)), device_id_type=MESH)

    loop(1, RING, greet)
    pl.semaphore_signal(barrier, inc=1, device_id=pair, device_id_type=MESH)
    pl.semaphore_wait(barrier, 31)

    def along(act):
        loop(1, RING, lambda i: act(lax.rem(z + i, RING)))

    def across(act):
        loop(1, RING, lambda i: act(lax.rem(me + i, RING)))

    def rise(i, h):
        block = rows_all.at[lax.rem(z + RING - i, RING), h]
        return remote(block, block, up_send.at[i, h], up_got.at[i, h], (s, above, y))

    def sink(i, h):
        block = rows_all.at[lax.rem(z + i, RING), h]
        return remote(block, block, down_send.at[i, h], down_got.at[i, h], (s, below, y))

    def risen(i, h):
        block = rows_all.at[lax.rem(z + RING - i, RING), h]
        return remote(block, block, up_send.at[i - 1, h], up_got.at[i - 1, h], (s, above, y))

    def sunk(i, h):
        block = rows_all.at[lax.rem(z + i, RING), h]
        return remote(block, block, down_send.at[i - 1, h], down_got.at[i - 1, h], (s, below, y))

    rows_all[z] = hn[...]
    names_all[z] = names[...]
    for h in range(2):
        rise(0, h).start()
        sink(0, h).start()

    def name_to(p):
        return remote(names, names_all.at[z], name_send.at[p], name_got.at[z], (s, p, y))

    def name_from(p):
        return remote(names, names_all.at[p], name_send.at[p], name_got.at[p], (s, p, y))

    along(lambda p: name_to(p).start())

    def ring_step(i):
        for h in range(2):
            risen(i, h).wait_recv()

            @pl.when(i < 8)
            def _():
                rise(i, h).start()

            @pl.when(i < 8)
            def _():
                sunk(i, h).wait_recv()

            @pl.when(i < 7)
            def _():
                sink(i, h).start()

    loop(1, 9, ring_step)
    along(lambda p: name_from(p).wait_recv())

    def product(b):
        columns = pl.ds(pl.multiple_of(b * 256, 256), 256)
        logits[:, columns] = dot(rows_all[:, 0].reshape(RING * FRAMES, HALF), weight[0:HALF, columns]) + dot(
            rows_all[:, 1].reshape(RING * FRAMES, HALF), weight[HALF:D, columns]
        )

    loop(0, WIDE // 256, product)

    columns = lax.broadcasted_iota(jnp.int32, (128, WIDE), 1)
    valid = columns[:FRAMES] < SHARD
    owned = jnp.where(columns < SHARD, columns + SHARD * z, -1).astype(F32)

    def selector(k):
        wanted = flip(jnp.broadcast_to(names_all[k, 0:1, :], (128, 128)))
        return (jnp.concatenate([wanted] * 4, axis=1) == owned).astype(F32)

    def frames_of(k):
        return pl.ds(pl.multiple_of(k * FRAMES, FRAMES), FRAMES)

    lane = lanes(FRAMES)

    def gather_stats(k):
        block = logits[frames_of(k), :]
        peak = jnp.max(jnp.where(valid, block, -jnp.inf), axis=1, keepdims=True)
        weightsum = jnp.sum(jnp.where(valid, jnp.exp(block - peak), 0.0), axis=1, keepdims=True)
        found = dot(block, selector(k), ((1,), (1,)), HIGHEST)
        stats[k] = pack(jnp.where(lane == 13, peak, jnp.where(lane == 14, weightsum, found)))

    loop(0, RING, gather_stats)
    stats_all[z] = stats[z]

    def stat_to(p):
        return remote(stats.at[p], stats_all.at[z], stat_send.at[p], stat_got.at[z], (s, p, y))

    def stat_from(p):
        return remote(stats.at[p], stats_all.at[p], stat_send.at[p], stat_got.at[p], (s, p, y))

    along(lambda p: stat_to(p).start())
    along(lambda p: stat_from(p).wait_recv())

    low = [stats_all[k] for k in range(RING)]
    high = [pltpu.roll(v, 64, 1) for v in low]
    peaks = functools.reduce(jnp.maximum, high)
    sums = sum(v * pltpu.roll(jnp.exp(v - peaks), 1, 0) for v in high)
    live = lanes(1) < FRAMES
    log_total = jnp.where(live, peaks[5:6] + jnp.log(jnp.where(live, sums[6:7], 1.0)), 0.0)
    both = jnp.concatenate([sum(low), sum(high)], axis=0)
    slot = lax.broadcasted_iota(jnp.int32, (16, 128), 0)
    both = jnp.where(lanes(16) < FRAMES, both - log_total, 0.0)
    both = jnp.where(slot < 13, both, jnp.where(slot == 14, log_total, 0.0))
    by_label = flip(both)
    row, col = lax.broadcasted_iota(jnp.int32, (128, 128), 0), lanes(128)
    odd = (col & 1) == 1
    expand = (col < 25) & (jnp.where(odd, col >> 1, 12) == row)
    expand = expand.astype(F32)
    emit[...] = dot(by_label[:FRAMES], expand, precision=HIGHEST)
    total_col = by_label[:FRAMES]
    one = lanes(1)
    span, last = meta[0:1, :], meta[1:2, :]
    jump, jump_back = meta[2:3, :] > 0, meta[3:4, :] > 0
    spot = one.astype(F32)
    ends = (spot == last) | (spot == last - 1.0)
    closing = jnp.where(ends, 0.0, LOG_ZERO)
    opening = jnp.where(one < 2, emit[0:1, :], LOG_ZERO)
    ahead[0:1, :] = opening
    behind[FRAMES - 1 : FRAMES, :] = closing

    def ctc_step(i, carry):
        a, b = carry
        once = jnp.where(one < 1, LOG_ZERO, pltpu.roll(a, 1, 1))
        twice = jnp.where(jump, pltpu.roll(a, 2, 1), LOG_ZERO)
        moved = triple(a, once, twice) + emit[pl.ds(i, 1), :]
        a = jnp.where(i.astype(F32) < span, moved, a)
        ahead[pl.ds(i, 1), :] = a
        t = FRAMES - 1 - i
        g = b + emit[pl.ds(t + 1, 1), :]
        once = jnp.where(one > 126, LOG_ZERO, pltpu.roll(g, 127, 1))
        twice = jnp.where(jump_back, pltpu.roll(g, 126, 1), LOG_ZERO)
        b = jnp.where(t.astype(F32) < span - 1.0, triple(g, once, twice), closing)
        behind[pl.ds(t, 1), :] = b
        return a, b

    final, _ = lax.fori_loop(1, FRAMES, ctc_step, (opening, closing))
    tail = jnp.where(ends, final, LOG_ZERO)
    top = jnp.max(tail, axis=1, keepdims=True)
    likely = top + jnp.log(jnp.sum(jnp.where(ends, jnp.exp(final - top), 0.0), axis=1, keepdims=True))
    loss_out[...] = jnp.broadcast_to(-likely, (8, 128))
    when = lax.broadcasted_iota(jnp.int32, (FRAMES, 128), 0).astype(F32)
    occupied = jnp.where(
        (when < span) & (lane < 25), -jnp.exp(ahead[...] + behind[...] - likely), 0.0
    )
    merged = dot(occupied, expand, ((1,), (1,)), HIGHEST)
    mass = jnp.sum(occupied, axis=1, keepdims=True)
    notes[...] = pack(
        jnp.where(lane == 13, mass, jnp.where(lane == 14, total_col, jnp.where(lane < 13, merged, 0.0)))
    )
    notes_all[z] = notes[...]

    def note_to(p):
        return remote(notes, notes_all.at[z], note_send.at[p], note_got.at[z], (s, p, y))

    def note_from(p):
        return remote(notes, notes_all.at[p], note_send.at[p], note_got.at[p], (s, p, y))

    along(lambda p: note_to(p).start())
    along(lambda p: note_from(p).wait_recv())

    def spread(k):
        packed = notes_all[k]
        known = flip(jnp.concatenate([packed, pltpu.roll(packed, 64, 1)], axis=0))[:FRAMES]
        scattered = dot(known, selector(k), precision=HIGHEST)
        block = logits[frames_of(k), :]
        value = scattered - jnp.exp(block - known[:, 14:15]) * known[:, 13:14]
        grads[frames_of(k), :] = jnp.where(valid, value, 0.0).astype(BF16)

    loop(0, RING, spread)
    for h in range(2):
        partial[:, HALF * h : HALF * (h + 1)] = dot(
            grads[...], rows_all[:, h].reshape(RING * FRAMES, HALF), ((0,), (0,))
        )

    def mine(core):
        return pl.ds(pl.multiple_of(256 * core, 256), 256)

    half_out[...] = partial[mine(1 - c), :].astype(BF16)
    swap = remote(half_out, half_in, half_send, half_got, pair)
    swap.start()
    swap.wait_recv()
    pieces[...] = (partial[mine(c), :] + half_in[...].astype(F32)).astype(BF16).reshape(RING, 16, D)

    def piece_to(p):
        return remote(pieces.at[p], pieces_all.at[me], piece_send.at[p], piece_got.at[me], chip(p))

    def piece_from(p):
        return remote(pieces.at[p], pieces_all.at[p], piece_send.at[p], piece_got.at[p], chip(p))

    across(lambda p: piece_to(p).start())
    pieces_all[me] = pieces[me]
    across(lambda p: piece_from(p).wait_recv())
    total[...] = sum(pieces_all[k].astype(F32) for k in range(RING)).astype(BF16)

    def total_to(p):
        return remote(total, totals.at[c, me], total_send.at[p], total_got.at[me], chip(p))

    def total_from(p):
        return remote(total, totals.at[c, p], total_send.at[p], total_got.at[p], chip(p))

    across(lambda p: total_to(p).start())
    totals[c, me] = total[...]
    across(lambda p: total_from(p).wait_recv())
    last_swap = remote(totals.at[c], totals.at[c], last_send, last_got, pair)
    last_swap.start()
    remote(totals.at[1 - c], totals.at[1 - c], last_send, last_got, pair).wait_recv()
    grad_out[...] = totals[...].reshape(WIDE, D)

    last_swap.wait_send()
    swap.wait_send()
    along(lambda p: name_to(p).wait_send())
    along(lambda p: stat_to(p).wait_send())
    along(lambda p: note_to(p).wait_send())
    across(lambda p: piece_to(p).wait_send())
    across(lambda p: total_to(p).wait_send())

    def ring_sent(i):
        for h in range(2):
            rise(i, h).wait_send()

            @pl.when(i < 7)
            def _():
                sink(i, h).wait_send()

    loop(0, 8, ring_sent)


def run_head(hn, weight, names, meta):
    local = pl.BlockSpec(memory_space=VMEM)
    return pl.pallas_call(
        head_kernel,
        out_shape=(jax.ShapeDtypeStruct((8, 128), F32), jax.ShapeDtypeStruct((WIDE, D), BF16)),
        in_specs=[local] * 4,
        out_specs=(local, local),
        scratch_shapes=[
            VMEM((RING, 2, FRAMES, HALF), BF16),
            VMEM((RING, 8, 128), F32),
            VMEM((RING * FRAMES, WIDE), F32),
            VMEM((RING, 8, 128), F32),
            VMEM((RING, 8, 128), F32),
            VMEM((FRAMES, 128), F32),
            VMEM((FRAMES, 128), F32),
            VMEM((FRAMES, 128), F32),
            VMEM((8, 128), F32),
            VMEM((RING, 8, 128), F32),
            VMEM((RING * FRAMES, WIDE), BF16),
            VMEM((WIDE, D), F32),
            VMEM((256, D), BF16),
            VMEM((256, D), BF16),
            VMEM((RING, 16, D), BF16),
            VMEM((RING, 16, D), BF16),
            VMEM((16, D), BF16),
            VMEM((2, RING, 16, D), BF16),
            DMA((8, 2)), DMA((8, 2)), DMA((8, 2)), DMA((8, 2)),
            DMA((RING,)), DMA((RING,)), DMA((RING,)), DMA((RING,)), DMA((RING,)), DMA((RING,)),
            DMA, DMA,
            DMA((RING,)), DMA((RING,)), DMA((RING,)), DMA((RING,)),
            DMA, DMA,
        ],
        compiler_params=pltpu.CompilerParams(
            collective_id=1, has_side_effects=True, vmem_limit_bytes=VMEM_LIMIT
        ),
    )(hn, weight, names, meta)


def per_device(
    frames,
    norm_gain,
    router,
    w_in,
    w_out,
    routing,
    head_gain,
    head_weight,
    frame_lengths,
    labels,
    label_lengths,
):
    section = lax.axis_index("section")
    micro = frames.shape[0]
    mine, which = section // 2, lax.rem(section, 2)
    block = lax.dynamic_index_in_dim(frames.reshape(micro, TOK, D), mine, 0, keepdims=False)
    routes = routing[0, :, :, :, 0].reshape(micro, TOK)
    same = routes[:, :, None] == routes[:, None, :]
    earlier = jnp.arange(TOK)[:, None] < jnp.arange(TOK)[None, :]
    rank = jnp.sum((same & earlier[None]).astype(jnp.int32), axis=1)
    spots = (8 * routes + rank).astype(F32)
    spots = jnp.pad(spots, ((0, 0), (0, D - TOK)), constant_values=-1.0)
    aux = jnp.concatenate([norm_gain, spots, jnp.zeros((3, D), F32)], axis=0)
    hn = run_moe(block, w_in[0, 0], w_out[0, 0], router[0].T, aux, head_gain.reshape(1, D))

    count = labels.shape[2]
    own = lax.dynamic_index_in_dim(labels.reshape(-1, count), section, 0, keepdims=False)
    span = lax.dynamic_index_in_dim(frame_lengths.reshape(-1), section, 0, keepdims=False)
    length = lax.dynamic_index_in_dim(label_lengths.reshape(-1), section, 0, keepdims=False)
    names = jnp.concatenate([own, jnp.zeros((1,), jnp.int32), jnp.full((115,), -2, jnp.int32)]).astype(F32)
    names = jnp.broadcast_to(names[None], (8, 128))
    ext = jnp.concatenate([jnp.stack([jnp.zeros_like(own), own], axis=1).reshape(-1), jnp.zeros((1,), jnp.int32)])
    skip = jnp.concatenate([jnp.zeros((2,), bool), (ext[2:] != 0) & (ext[2:] != ext[:-2])])
    skip = jnp.pad(skip.astype(F32), (0, 128 - skip.shape[0]))
    skip_back = jnp.concatenate([skip[2:], jnp.zeros((2,), F32)])
    meta = jnp.stack(
        [jnp.full((128,), span).astype(F32), jnp.full((128,), 2 * length).astype(F32), skip, skip_back]
        + [jnp.zeros((128,), F32)] * 4
    )
    weight = jnp.pad(head_weight, ((0, 0), (0, WIDE - head_weight.shape[1])))
    losses, grad = run_head(hn, weight, names, meta)
    return losses[0:1, 0:1], grad[: head_weight.shape[1]].T


def solution(mesh):
    placed = (
        P(None, ("expert", "dp"), None, None),
        P("section", None),
        P("section", None, None),
        P("section", "expert", None, None),
        P("section", "expert", None, None),
        P("section", None, ("expert", "dp"), None, None),
        P(),
        P(None, "expert"),
        P(None, ("expert", "dp")),
        P(None, ("expert", "dp"), None),
        P(None, ("expert", "dp")),
    )
    return jax.shard_map(
        per_device,
        mesh=mesh,
        in_specs=placed,
        out_specs=(P("section", ("expert", "dp")), P(None, "expert")),
        check_vma=False,
    )
```

time: 1300 us -> 387 us (0.30)
  blocking collectives: 481 us -> 0 us
  waiting for transfers between devices: 381 us -> 0 us
  Pallas kernels: 0 us -> 366 us
  starting transfers between devices: 198 us -> 0 us
  loops' own time: 62 us -> 0 us
  other arithmetic: 53.9 us -> 3.19 us
  local copies, waits for them, and re-layouts: 65.4 us -> 15.4 us
  matrix products: 31.6 us -> 0 us
  between operations: 22.4 us -> 2.02 us
    pallas_call x0 -> x2, Pallas kernels: none -> 366 us  [the longest x1 257 us: run_moe(): pl.pallas_call(moe_kernel, out_shape=jax.ShapeDtypeStruct((2, FRAMES, HAL...]
    all_to_all x11 -> x0, blocking collectives: 230 us -> none  [section_layer(): lax.all_to_all(outgoing, 'expert', split_axis=0, concat_axis=0, tiled=True)]
    psum x2 -> x0, blocking collectives: 184 us -> none  [the longest x1 164 us: per_device(): head_grad = lax.psum(partial_grad, ('section', 'dp')).astype(jnp.bfloat16)]
    all_to_all x11 -> x0, waiting for transfers between devices: 156 us -> none  [section_layer(): lax.all_to_all(processed, 'expert', split_axis=0, concat_axis=0, tiled=True)]
    ppermute x10 -> x0, starting transfers between devices: 122 us -> none  [shifted(): return lax.ppermute(value, axis, pairs)]
    psum x1 -> x0, waiting for transfers between devices: 79.8 us -> none  [from_root(): return lax.psum(block, axis)]
    reduce_scatter x1 -> x0, waiting for transfers between devices: 76.2 us -> none  [per_device(): lax.psum_scatter(emission_part, 'expert', scatter_dimension=0, tiled=True)]
    all_to_all x11 -> x0, starting transfers between devices: 75.4 us -> none  [section_layer(): lax.all_to_all(processed, 'expert', split_axis=0, concat_axis=0, tiled=True)]
  transfers between devices with their start and end apart: 24 -> 0, of which waited for: 24 -> 0; matrix products, arithmetic and copies ran while one was open for 1% -> 0% of each run, Pallas kernels for 0% -> 0%
where the time goes in v1:
time: 387 us
  Pallas kernels  366 us (95%)
  local copies, waits for them, and re-layouts  15.4 us (4%)
    pallas_call x1, Pallas kernels, run_moe(): pl.pallas_call(moe_kernel, out_shape=jax.ShapeDtypeStruct((2, FRAMES, HAL...  257 us
    pallas_call x1, Pallas kernels, run_head(): pl.pallas_call(head_kernel, out_shape=(jax.ShapeDtypeStruct((8, 128), F32...  109 us

profile of v1, /device:TPU:1, one launch (start us, length us, event | category | flops | bytes accessed | tf_op | source)
XLA Modules:
  0.0 386.9 jit_solution(10910763081531804227)
XLA Ops:
  0.7 1.2 copy-done
  1.8 0.1 pad.29.clone
  1.9 0.7 fusion.2
  2.6 0.1 add_convert_fusion.1
  2.7 0.8 copy.22
  3.5 0.1 reshape.62
  3.5 0.6 dynamic_slice.17
  4.8 0.8 copy.23
  5.6 0.1 reshape.63
  5.6 0.6 dynamic_slice.18
  6.9 0.6 broadcast_in_dim.8.names
  7.5 0.5 broadcast.47
  8.0 1.4 reduce.3
  9.3 0.1 reshape_squeeze.3
  9.4 1.3 reshape.60.head_gain
  10.7 0.1 copy.25
  10.8 0.1 stack.27.clone
  10.9 0.1 reshape.64
  11.0 0.1 pad_add_fusion
  11.1 0.1 compare_and_fusion
  11.1 0.1 pad_convert_fusion
  11.2 0.1 slice.18
  11.3 0.6 stack.31.meta
  11.9 0.1 convert_reduce_fusion
  12.1 1.4 fusion.aux
  13.4 0.7 dynamic-slice_bitcast_fusion.x0
  14.2 257.3 %shard_map.122.hn = bf16[2,48,640]{2,1,0:T(8,128)(2,1)} custom-call(bf16[96,1280]{1,0:T(8,128)(2,1)} %dynamic-slice_bitcast_fusion.x0, bf16[1280,256]{1,0:T(8,128)(2,1)} %bitcast.23, bf16[256,1280]{1,0:T(8,128)(2,1)} %bitcast.24, bf16[16,1280]{1,0:T(8,128)(2,1)} %bitcast.25, f32[8,1280]{1,0:T(8,128)} %fusion.aux, f32[1,1280]{1,0:T(1,128)} %reshape.60.head_gain), custom_call_target="tpu_custom_call" | custom-call | tf_op jit(solution)/shard_map/pallas_call | solution.py:346
  271.5 1.6 copy.21
  273.1 1.2 pad.19.weight
  274.4 108.9 %shard_map.123 = (f32[8,128]{1,0:T(8,128)}, bf16[512,1280]{1,0:T(8,128)(2,1)}) custom-call(bf16[2,48,640]{2,1,0:T(8,128)(2,1)} %shard_map.122.hn, bf16[1280,512]{1,0:T(8,128)(2,1)} %pad.19.weight, f32[8,128]{1,0:T(8,128)} %broadcast_in_dim.8.names, f32[8,128]{1,0:T(8,128)} %stack.31.meta), custom_call_target="tpu_custom_call" | custom-call | tf_op jit(solution)/shard_map/pallas_call | solution.py:653
  383.3 1.2 slice.19
  384.5 2.4 slice_bitcast_fusion
  (9 shorter events, 0.0 us)
Async XLA Ops:
  0.6 1.2 copy-start

commit v2 on v1

--- a/solution.py
+++ b/solution.py
@@ -12,10 +12,13 @@
 MESH = pl.DeviceIdType.MESH
 F32, BF16 = jnp.float32, jnp.bfloat16
 D, HALF, EFF, LAYERS, RING, TOK, FRAMES = 1280, 640, 256, 8, 16, 96, 48
-PIECES = 8
+PIECES = 16
+SKEW = 3
+TURNS = PIECES // 4
 CHUNKS = LAYERS * PIECES
 IN_ROWS, OUT_ROWS = D // PIECES, EFF // PIECES
 SHARD, WIDE = 500, 512
+PART = D // RING
 HIGHEST = lax.Precision.HIGHEST
 VMEM = pltpu.VMEM
 DMA = pltpu.SemaphoreType.DMA
@@ -50,10 +53,10 @@
 
 
 def moe_kernel(
-    x0, w_in, w_out, router, aux, head_gain, hn_out,
-    win, wout, routers, auxes, state, give, take, answer, back, stage_in, stage_out, passed, landed,
+    frames, w_in, w_out, router, gain, routes, head_gain, hn_out,
+    win, wout, aux, routers, auxes, state, give, take, answer, back, stage_in, stage_out, passed, landed,
     got_in, got_out, on_in, on_out, copy_in, copy_out, have_in, have_out,
-    lay_send, stage_send, stage_got, small_send, small_got, give_send, take_got, answer_send, back_got, hn_send, hn_got,
+    lay_send, stage_send, stage_got, small_send, small_got, give_send, take_got, answer_send, back_got, hn_send, hn_got, state_got,
 ):
     s, x, c, z, y = coords()
     me = 4 * x + y
@@ -71,10 +74,10 @@
     pl.semaphore_wait(barrier, 33)
 
     def in_rows(j):
-        return pl.ds(pl.multiple_of(j * IN_ROWS, 32), IN_ROWS)
+        return pl.ds(pl.multiple_of(j * IN_ROWS, 16), IN_ROWS)
 
     def out_rows(j):
-        return pl.ds(pl.multiple_of(j * OUT_ROWS, 32), OUT_ROWS)
+        return pl.ds(pl.multiple_of(j * OUT_ROWS, 16), OUT_ROWS)
 
     def share(layer, i, src_in, src_out):
         j = y + 4 * i
@@ -108,13 +111,23 @@
 
     @pl.when((c == 0) & (x == 0))
     def _():
-        for i in range(2):
+        for i in range(TURNS):
             each(share(0, i, w_in.at[in_rows(y + 4 * i)], w_out.at[out_rows(y + 4 * i)]), start)
 
     @pl.when((c == 0) & (x > 0))
     def _():
-        for i in range(2):
+        for i in range(TURNS):
             each(staged(i), start)
+
+    rows, cols = lax.broadcasted_iota(jnp.int32, (128, 128), 0), lax.broadcasted_iota(jnp.int32, (128, 128), 1)
+    aux[...] = jnp.zeros_like(aux)
+    aux[0:1, :] = gain[...]
+    for m in range(4):
+        named = jnp.broadcast_to(routes[m : m + 1, :], (128, 128))
+        before = (jnp.transpose(named) == named) & (rows < cols)
+        rank = jnp.sum(before.astype(F32), axis=0, keepdims=True)
+        live = lax.broadcasted_iota(jnp.int32, (1, 128), 1) < TOK
+        aux[m + 1 : m + 2, 0:128] = jnp.where(live, 8.0 * routes[m : m + 1, :] + rank, -1.0)
 
     for gap in range(1, 4):
         each(small(lax.rem(x + gap, 4)), start)
@@ -138,7 +151,7 @@
         up, down = lax.rem(z + RING - me, RING), lax.rem(me + RING - z, RING)
 
         def distribute(layer, slot, pick):
-            for i in range(2):
+            for i in range(TURNS):
                 j = y + 4 * i
                 src_in, src_out = pick(i)
 
@@ -170,12 +183,12 @@
         def rise(k):
             layer, j = k // PIECES, lax.rem(k, PIECES)
             ref = win.at[layer, in_rows(j)]
-            return remote(ref, ref, on_in.at[k], got_in.at[k], (s, above, y))
+            return remote(ref, ref, on_in, got_in.at[k], (s, above, y))
 
         def sink(k):
             layer, j = k // PIECES, lax.rem(k, PIECES)
             ref = wout.at[layer, out_rows(j)]
-            return remote(ref, ref, on_out.at[k], got_out.at[k], (s, below, y))
+            return remote(ref, ref, on_out, got_out.at[k], (s, below, y))
 
         def hand_in(layer):
             return remote(win.at[layer], win.at[layer], copy_in.at[layer], have_in.at[layer], (s - 1, z, y))
@@ -184,17 +197,17 @@
             return remote(wout.at[layer], wout.at[layer], copy_out.at[layer], have_out.at[layer], (s - 1, z, y))
 
         def tick(t):
-            @pl.when((x > 0) & (t == 16 * x - 8))
+            @pl.when((x > 0) & (t == PIECES * (2 * x - 1)))
             def _():
-                for i in range(2):
+                for i in range(TURNS):
                     each(staged(i), got)
                 distribute(2 * x, 0, from_stage)
 
-            @pl.when(t == 16 * x)
+            @pl.when(t == 2 * PIECES * x)
             def _():
                 distribute(2 * x + 1, 1, from_own)
 
-            ku, kd = t - up, t - down
+            ku, kd = t - SKEW * up, t - SKEW * down
 
             @pl.when((ku >= 0) & (ku < CHUNKS))
             def _():
@@ -220,11 +233,11 @@
                 def _():
                     hand_out(kd // PIECES).start()
 
-        loop(0, CHUNKS + RING - 1, tick)
+        loop(0, CHUNKS + SKEW * (RING - 1), tick)
 
         @pl.when(jnp.logical_not(at_home))
         def _():
-            for i in range(2):
+            for i in range(TURNS):
                 @pl.when(x > 0)
                 def _():
                     each(carried(2 * x, 0, i, *from_stage(i)), sent)
@@ -233,11 +246,11 @@
 
         @pl.when(up < RING - 1)
         def _():
-            loop(0, CHUNKS, lambda k: rise(k).wait_send())
+            pltpu.make_async_copy(win, win, on_in).wait()
 
         @pl.when(down < RING - 1)
         def _():
-            loop(0, CHUNKS, lambda k: sink(k).wait_send())
+            pltpu.make_async_copy(wout, wout, on_out).wait()
 
         loop(0, LAYERS, lambda layer: hand_in(layer).wait_send())
         loop(0, LAYERS, lambda layer: hand_out(layer).wait_send())
@@ -245,31 +258,31 @@
 
     @pl.when(c == 0)
     def _():
-        state[...] = x0[...]
+        pltpu.make_async_copy(frames.at[x], state, state_got).start()
 
         def smalls(layer):
             pltpu.make_async_copy(aux, auxes.at[layer], small_got.at[0, layer]).wait()
             pltpu.make_async_copy(router, routers.at[layer], small_got.at[1, layer]).wait()
 
         loop(0, LAYERS, smalls)
+        pltpu.make_async_copy(frames.at[x], state, state_got).wait()
 
         def chip(p):
             return (2 * (p // 4), z, lax.rem(p, 4))
 
         def out_to(p):
-            return remote(give.at[p], take.at[me], give_send.at[p], take_got.at[me], chip(p))
-
-        def in_from(p):
-            return remote(give.at[p], take.at[p], give_send.at[p], take_got.at[p], chip(p))
+            return remote(give.at[p], take.at[me], give_send, take_got, chip(p))
 
         def back_to(p):
-            return remote(answer.at[p], back.at[me], answer_send.at[p], back_got.at[me], chip(p))
-
-        def back_from(p):
-            return remote(answer.at[p], back.at[p], answer_send.at[p], back_got.at[p], chip(p))
-
-        def others(act):
-            loop(1, RING, lambda i: act(lax.rem(me + i, RING)))
+            return remote(answer.at[p], back.at[me], answer_send, back_got, chip(p))
+
+        def start_all(copy):
+            for i in range(1, RING):
+                copy(lax.rem(me + i, RING)).start()
+
+        def wait_all(buffer, sem):
+            most = buffer.at[pl.ds(0, RING - 1)]
+            pltpu.make_async_copy(most, most, sem).wait()
 
         def layer_step(layer):
             xf = state[...].astype(F32)
@@ -281,7 +294,7 @@
             left = dot(pick, normed[:, :HALF]).reshape(RING, 8, HALF)
             right = dot(pick, normed[:, HALF:]).reshape(RING, 8, HALF)
             give[...] = jnp.concatenate([left, right], axis=1).astype(BF16)
-            others(lambda p: out_to(p).start())
+            start_all(out_to)
             take[me] = give[me]
 
             columns = jnp.transpose(jnp.broadcast_to(spots, (128, 128)))[:TOK, :].astype(jnp.int32)
@@ -295,7 +308,7 @@
             put_right = jnp.concatenate(spread[2:], axis=1)
 
             pltpu.make_async_copy(win.at[layer], win.at[layer], have_in.at[layer]).wait()
-            others(lambda p: in_from(p).wait_recv())
+            wait_all(take, take_got)
             rows = take[...].reshape(RING * 16, HALF)
             first = dot(rows, win[layer, 0:HALF, :]).reshape(RING, 16, EFF)
             second = dot(rows, win[layer, HALF:D, :]).reshape(RING, 16, EFF)
@@ -304,14 +317,14 @@
             pltpu.make_async_copy(wout.at[layer], wout.at[layer], have_out.at[layer]).wait()
             result = dot(active, wout[layer]).reshape(RING, 8, D)
             answer[...] = jnp.concatenate([result[:, :, :HALF], result[:, :, HALF:]], axis=1).astype(BF16)
-            others(lambda p: back_to(p).start())
+            start_all(back_to)
             back[me] = answer[me]
-            others(lambda p: out_to(p).wait_send())
-            others(lambda p: back_from(p).wait_recv())
+            wait_all(give, give_send)
+            wait_all(back, back_got)
             returned = back[...].reshape(RING * 16, HALF)
             mixed = jnp.concatenate([dot(put_left, returned), dot(put_right, returned)], axis=1)
             state[...] = (xf + gate * mixed).astype(BF16)
-            others(lambda p: back_to(p).wait_send())
+            wait_all(answer, answer_send)
 
         loop(0, LAYERS, layer_step)
         hn = rms(state[...].astype(F32), head_gain[...])
@@ -322,12 +335,12 @@
 
         @pl.when(x == 0)
         def _():
-            for i in range(2):
+            for i in range(TURNS):
                 each(share(0, i, w_in.at[in_rows(y + 4 * i)], w_out.at[out_rows(y + 4 * i)]), sent)
 
         @pl.when(x > 0)
         def _():
-            for i in range(2):
+            for i in range(TURNS):
                 each(staged(i), sent)
 
         remote(passed, landed, hn_send, hn_got, (s + 1, z, y)).wait_send()
@@ -341,16 +354,17 @@
         each(small(lax.rem(x + gap, 4)), sent)
 
 
-def run_moe(x0, w_in, w_out, router, aux, head_gain):
+def run_moe(frames, w_in, w_out, router, gain, routes, head_gain):
     anywhere, local = pl.BlockSpec(memory_space=pl.ANY), pl.BlockSpec(memory_space=VMEM)
     return pl.pallas_call(
         moe_kernel,
         out_shape=jax.ShapeDtypeStruct((2, FRAMES, HALF), BF16),
-        in_specs=[local, anywhere, anywhere, local, local, local],
+        in_specs=[anywhere, anywhere, anywhere, local, local, local, local],
         out_specs=local,
         scratch_shapes=[
             VMEM((LAYERS, D, EFF), BF16),
             VMEM((LAYERS, EFF, D), BF16),
+            VMEM((8, D), F32),
             VMEM((LAYERS, 16, D), BF16),
             VMEM((LAYERS, 8, D), F32),
             VMEM((TOK, D), BF16),
@@ -358,20 +372,20 @@
             VMEM((RING, 16, HALF), BF16),
             VMEM((RING, 16, HALF), BF16),
             VMEM((RING, 16, HALF), BF16),
-            VMEM((2, IN_ROWS, EFF), BF16),
-            VMEM((2, OUT_ROWS, D), BF16),
+            VMEM((TURNS, IN_ROWS, EFF), BF16),
+            VMEM((TURNS, OUT_ROWS, D), BF16),
             VMEM((2, FRAMES, HALF), BF16),
             VMEM((2, FRAMES, HALF), BF16),
-            DMA((CHUNKS,)), DMA((CHUNKS,)), DMA((CHUNKS,)), DMA((CHUNKS,)),
+            DMA((CHUNKS,)), DMA((CHUNKS,)), DMA, DMA,
             DMA((LAYERS,)), DMA((LAYERS,)), DMA((LAYERS,)), DMA((LAYERS,)),
-            DMA((4, 2)), DMA((2, 2)), DMA((2, 2)), DMA((2, 4)), DMA((2, LAYERS)),
-            DMA((RING,)), DMA((RING,)), DMA((RING,)), DMA((RING,)),
-            DMA, DMA,
+            DMA((4, TURNS)), DMA((2, TURNS)), DMA((2, TURNS)), DMA((2, 4)), DMA((2, LAYERS)),
+            DMA, DMA, DMA, DMA,
+            DMA, DMA, DMA,
         ],
         compiler_params=pltpu.CompilerParams(
             collective_id=0, has_side_effects=True, vmem_limit_bytes=VMEM_LIMIT
         ),
-    )(x0, w_in, w_out, router, aux, head_gain)
+    )(frames, w_in, w_out, router, gain, routes, head_gain)
 
 
 def flip(block):
@@ -396,8 +410,8 @@
 
 
 def head_kernel(
-    hn, weight, names, meta, loss_out, grad_out,
-    rows_all, names_all, logits, stats, stats_all, emit, ahead, behind, notes, notes_all, grads, partial,
+    hn, weight, numbers, loss_out, grad_out,
+    rows_all, names, names_all, logits, stats, stats_all, emit, ahead, behind, notes, notes_all, grads, partial,
     half_out, half_in, pieces, pieces_all, total, totals,
     up_send, up_got, down_send, down_got, name_send, name_got, stat_send, stat_got, note_send, note_got,
     half_send, half_got, piece_send, piece_got, total_send, total_got, last_send, last_got,
@@ -420,10 +434,12 @@
     pl.semaphore_wait(barrier, 31)
 
     def along(act):
-        loop(1, RING, lambda i: act(lax.rem(z + i, RING)))
+        for i in range(1, RING):
+            act(lax.rem(z + i, RING))
 
     def across(act):
-        loop(1, RING, lambda i: act(lax.rem(me + i, RING)))
+        for i in range(1, RING):
+            act(lax.rem(me + i, RING))
 
     def rise(i, h):
         block = rows_all.at[lax.rem(z + RING - i, RING), h]
@@ -442,18 +458,65 @@
         return remote(block, block, down_send.at[i - 1, h], down_got.at[i - 1, h], (s, below, y))
 
     rows_all[z] = hn[...]
-    names_all[z] = names[...]
     for h in range(2):
         rise(0, h).start()
         sink(0, h).start()
 
+    one = lanes(1)
+    chosen = lax.broadcasted_iota(jnp.int32, (8, 128), 0) == s
+    known_row = jnp.sum(jnp.where(chosen, numbers[...], 0.0), axis=0, keepdims=True)
+    tags = jnp.where(one < 12, known_row, jnp.where(one == 12, 0.0, -2.0))
+    names[...] = jnp.broadcast_to(tags, (8, 128))
+
+    def all_but_one(buffer, sem):
+        most = buffer.at[pl.ds(0, RING - 1)]
+        pltpu.make_async_copy(most, most, sem).wait()
+
     def name_to(p):
-        return remote(names, names_all.at[z], name_send.at[p], name_got.at[z], (s, p, y))
-
-    def name_from(p):
-        return remote(names, names_all.at[p], name_send.at[p], name_got.at[p], (s, p, y))
+        return remote(names, names_all.at[z], name_send, name_got, (s, p, y))
 
     along(lambda p: name_to(p).start())
+    names_all[z] = names[...]
+    logits[:, WIDE - 128 : WIDE] = jnp.zeros((RING * FRAMES, 128), F32)
+
+    columns = lax.broadcasted_iota(jnp.int32, (128, WIDE), 1)
+    valid = columns[:FRAMES] < SHARD
+    owned = jnp.where(columns < SHARD, columns + SHARD * z, -1).astype(F32)
+
+    def selector(k):
+        wanted = flip(jnp.broadcast_to(names_all[k, 0:1, :], (128, 128)))
+        return (jnp.concatenate([wanted] * 4, axis=1) == owned).astype(F32).astype(BF16)
+
+    def thirds(value):
+        high = value.astype(BF16)
+        rest = value - high.astype(F32)
+        middle = rest.astype(BF16)
+        return jnp.concatenate([high, middle, (rest - middle.astype(F32)).astype(BF16)], axis=0)
+
+    def joined(parts):
+        return parts[0:FRAMES] + parts[FRAMES : 2 * FRAMES] + parts[2 * FRAMES :]
+
+    def frames_of(k):
+        return pl.ds(pl.multiple_of(k * FRAMES, FRAMES), FRAMES)
+
+    lane = lanes(FRAMES)
+
+    def stat_to(p):
+        return remote(stats.at[p], stats_all.at[z], stat_send, stat_got, (s, p, y))
+
+    def evaluate(blocks):
+        def side(h):
+            return jnp.concatenate([rows_all[k, h] for k in blocks], axis=0)
+
+        value = dot(side(0), weight[0:HALF, :]) + dot(side(1), weight[HALF:D, :])
+        for n, k in enumerate(blocks):
+            logits[frames_of(k), 0:SHARD] = value[n * FRAMES : (n + 1) * FRAMES]
+        for k in blocks:
+            block = logits[frames_of(k), :]
+            peak = jnp.max(jnp.where(valid, block, -jnp.inf), axis=1, keepdims=True)
+            weightsum = jnp.sum(jnp.where(valid, jnp.exp(block - peak), 0.0), axis=1, keepdims=True)
+            found = joined(dot(thirds(block), selector(k), ((1,), (1,))))
+            stats[k] = pack(jnp.where(lane == 13, peak, jnp.where(lane == 14, weightsum, found)))
 
     def ring_step(i):
         for h in range(2):
@@ -462,57 +525,30 @@
             @pl.when(i < 8)
             def _():
                 rise(i, h).start()
-
-            @pl.when(i < 8)
-            def _():
                 sunk(i, h).wait_recv()
 
             @pl.when(i < 7)
             def _():
                 sink(i, h).start()
 
+        @pl.when(i == 1)
+        def _():
+            all_but_one(names_all, name_got)
+
+        lower, upper = lax.rem(z + RING + 1 - i, RING), lax.rem(z + i - 1, RING)
+        evaluate((lower, upper))
+
+        @pl.when(i > 1)
+        def _():
+            stat_to(lower).start()
+            stat_to(upper).start()
+
     loop(1, 9, ring_step)
-    along(lambda p: name_from(p).wait_recv())
-
-    def product(b):
-        columns = pl.ds(pl.multiple_of(b * 256, 256), 256)
-        logits[:, columns] = dot(rows_all[:, 0].reshape(RING * FRAMES, HALF), weight[0:HALF, columns]) + dot(
-            rows_all[:, 1].reshape(RING * FRAMES, HALF), weight[HALF:D, columns]
-        )
-
-    loop(0, WIDE // 256, product)
-
-    columns = lax.broadcasted_iota(jnp.int32, (128, WIDE), 1)
-    valid = columns[:FRAMES] < SHARD
-    owned = jnp.where(columns < SHARD, columns + SHARD * z, -1).astype(F32)
-
-    def selector(k):
-        wanted = flip(jnp.broadcast_to(names_all[k, 0:1, :], (128, 128)))
-        return (jnp.concatenate([wanted] * 4, axis=1) == owned).astype(F32)
-
-    def frames_of(k):
-        return pl.ds(pl.multiple_of(k * FRAMES, FRAMES), FRAMES)
-
-    lane = lanes(FRAMES)
-
-    def gather_stats(k):
-        block = logits[frames_of(k), :]
-        peak = jnp.max(jnp.where(valid, block, -jnp.inf), axis=1, keepdims=True)
-        weightsum = jnp.sum(jnp.where(valid, jnp.exp(block - peak), 0.0), axis=1, keepdims=True)
-        found = dot(block, selector(k), ((1,), (1,)), HIGHEST)
-        stats[k] = pack(jnp.where(lane == 13, peak, jnp.where(lane == 14, weightsum, found)))
-
-    loop(0, RING, gather_stats)
+    opposite = lax.rem(z + 8, RING)
+    evaluate((opposite,))
+    stat_to(opposite).start()
     stats_all[z] = stats[z]
-
-    def stat_to(p):
-        return remote(stats.at[p], stats_all.at[z], stat_send.at[p], stat_got.at[z], (s, p, y))
-
-    def stat_from(p):
-        return remote(stats.at[p], stats_all.at[p], stat_send.at[p], stat_got.at[p], (s, p, y))
-
-    along(lambda p: stat_to(p).start())
-    along(lambda p: stat_from(p).wait_recv())
+    all_but_one(stats_all, stat_got)
 
     low = [stats_all[k] for k in range(RING)]
     high = [pltpu.roll(v, 64, 1) for v in low]
@@ -531,9 +567,11 @@
     expand = expand.astype(F32)
     emit[...] = dot(by_label[:FRAMES], expand, precision=HIGHEST)
     total_col = by_label[:FRAMES]
-    one = lanes(1)
-    span, last = meta[0:1, :], meta[1:2, :]
-    jump, jump_back = meta[2:3, :] > 0, meta[3:4, :] > 0
+    span = jnp.sum(jnp.where(one == 12, known_row, 0.0), axis=1, keepdims=True)
+    last = 2.0 * jnp.sum(jnp.where(one == 13, known_row, 0.0), axis=1, keepdims=True)
+    differs = (known_row != pltpu.roll(known_row, 1, 1)) & (known_row != 0.0) & (one > 0) & (one < 12)
+    jumps = dot(jnp.broadcast_to(differs.astype(F32), (8, 128)), expand)[0:1]
+    jump, jump_back = jumps > 0.5, pltpu.roll(jumps, 126, 1) > 0.5
     spot = one.astype(F32)
     ends = (spot == last) | (spot == last - 1.0)
     closing = jnp.where(ends, 0.0, LOG_ZERO)
@@ -573,69 +611,62 @@
     notes_all[z] = notes[...]
 
     def note_to(p):
-        return remote(notes, notes_all.at[z], note_send.at[p], note_got.at[z], (s, p, y))
-
-    def note_from(p):
-        return remote(notes, notes_all.at[p], note_send.at[p], note_got.at[p], (s, p, y))
+        return remote(notes, notes_all.at[z], note_send, note_got, (s, p, y))
 
     along(lambda p: note_to(p).start())
-    along(lambda p: note_from(p).wait_recv())
-
-    def spread(k):
-        packed = notes_all[k]
-        known = flip(jnp.concatenate([packed, pltpu.roll(packed, 64, 1)], axis=0))[:FRAMES]
-        scattered = dot(known, selector(k), precision=HIGHEST)
-        block = logits[frames_of(k), :]
-        value = scattered - jnp.exp(block - known[:, 14:15]) * known[:, 13:14]
-        grads[frames_of(k), :] = jnp.where(valid, value, 0.0).astype(BF16)
-
-    loop(0, RING, spread)
+    all_but_one(notes_all, note_got)
+
+    def spread(pair_at):
+        for k in (2 * pair_at, 2 * pair_at + 1):
+            packed = notes_all[k]
+            known = flip(jnp.concatenate([packed, pltpu.roll(packed, 64, 1)], axis=0))[:FRAMES]
+            scattered = joined(dot(thirds(known), selector(k)))
+            block = logits[frames_of(k), :]
+            value = scattered - jnp.exp(block - known[:, 14:15]) * known[:, 13:14]
+            grads[frames_of(k), :] = jnp.where(valid, value, 0.0).astype(BF16)
+
+    loop(0, RING // 2, spread)
     for h in range(2):
-        partial[:, HALF * h : HALF * (h + 1)] = dot(
-            grads[...], rows_all[:, h].reshape(RING * FRAMES, HALF), ((0,), (0,))
+        partial[HALF * h : HALF * (h + 1), :] = dot(
+            rows_all[:, h].reshape(RING * FRAMES, HALF), grads[...], ((0,), (0,))
         )
 
     def mine(core):
         return pl.ds(pl.multiple_of(256 * core, 256), 256)
 
-    half_out[...] = partial[mine(1 - c), :].astype(BF16)
+    half_out[...] = partial[:, mine(1 - c)].astype(BF16)
     swap = remote(half_out, half_in, half_send, half_got, pair)
     swap.start()
     swap.wait_recv()
-    pieces[...] = (partial[mine(c), :] + half_in[...].astype(F32)).astype(BF16).reshape(RING, 16, D)
+    pieces[...] = (partial[:, mine(c)] + half_in[...].astype(F32)).astype(BF16).reshape(RING, PART, 256)
 
     def piece_to(p):
-        return remote(pieces.at[p], pieces_all.at[me], piece_send.at[p], piece_got.at[me], chip(p))
-
-    def piece_from(p):
-        return remote(pieces.at[p], pieces_all.at[p], piece_send.at[p], piece_got.at[p], chip(p))
+        return remote(pieces.at[p], pieces_all.at[me], piece_send, piece_got, chip(p))
 
     across(lambda p: piece_to(p).start())
     pieces_all[me] = pieces[me]
-    across(lambda p: piece_from(p).wait_recv())
+    all_but_one(pieces_all, piece_got)
     total[...] = sum(pieces_all[k].astype(F32) for k in range(RING)).astype(BF16)
 
     def total_to(p):
-        return remote(total, totals.at[c, me], total_send.at[p], total_got.at[me], chip(p))
-
-    def total_from(p):
-        return remote(total, totals.at[c, p], total_send.at[p], total_got.at[p], chip(p))
+        return remote(total, totals.at[c, me], total_send, total_got, chip(p))
 
     across(lambda p: total_to(p).start())
     totals[c, me] = total[...]
-    across(lambda p: total_from(p).wait_recv())
+    all_but_one(totals.at[c], total_got)
     last_swap = remote(totals.at[c], totals.at[c], last_send, last_got, pair)
     last_swap.start()
     remote(totals.at[1 - c], totals.at[1 - c], last_send, last_got, pair).wait_recv()
-    grad_out[...] = totals[...].reshape(WIDE, D)
+    grad_out[:, 0:256] = totals[0].reshape(D, 256)
+    grad_out[:, 256:SHARD] = totals[1].reshape(D, 256)[:, : SHARD - 256]
 
     last_swap.wait_send()
     swap.wait_send()
-    along(lambda p: name_to(p).wait_send())
-    along(lambda p: stat_to(p).wait_send())
-    along(lambda p: note_to(p).wait_send())
-    across(lambda p: piece_to(p).wait_send())
-    across(lambda p: total_to(p).wait_send())
+    all_but_one(names_all, name_send)
+    all_but_one(stats, stat_send)
+    all_but_one(notes_all, note_send)
+    all_but_one(pieces, piece_send)
+    all_but_one(pieces, total_send)
 
     def ring_sent(i):
         for h in range(2):
@@ -648,15 +679,16 @@
     loop(0, 8, ring_sent)
 
 
-def run_head(hn, weight, names, meta):
+def run_head(hn, weight, numbers):
     local = pl.BlockSpec(memory_space=VMEM)
     return pl.pallas_call(
         head_kernel,
-        out_shape=(jax.ShapeDtypeStruct((8, 128), F32), jax.ShapeDtypeStruct((WIDE, D), BF16)),
-        in_specs=[local] * 4,
+        out_shape=(jax.ShapeDtypeStruct((8, 128), F32), jax.ShapeDtypeStruct((D, SHARD), BF16)),
+        in_specs=[local] * 3,
         out_specs=(local, local),
         scratch_shapes=[
             VMEM((RING, 2, FRAMES, HALF), BF16),
+            VMEM((8, 128), F32),
             VMEM((RING, 8, 128), F32),
             VMEM((RING * FRAMES, WIDE), F32),
             VMEM((RING, 8, 128), F32),
@@ -667,23 +699,23 @@
             VMEM((8, 128), F32),
             VMEM((RING, 8, 128), F32),
             VMEM((RING * FRAMES, WIDE), BF16),
-            VMEM((WIDE, D), F32),
-            VMEM((256, D), BF16),
-            VMEM((256, D), BF16),
-            VMEM((RING, 16, D), BF16),
-            VMEM((RING, 16, D), BF16),
-            VMEM((16, D), BF16),
-            VMEM((2, RING, 16, D), BF16),
+            VMEM((D, WIDE), F32),
+            VMEM((D, 256), BF16),
+            VMEM((D, 256), BF16),
+            VMEM((RING, PART, 256), BF16),
+            VMEM((RING, PART, 256), BF16),
+            VMEM((PART, 256), BF16),
+            VMEM((2, RING, PART, 256), BF16),
             DMA((8, 2)), DMA((8, 2)), DMA((8, 2)), DMA((8, 2)),
-            DMA((RING,)), DMA((RING,)), DMA((RING,)), DMA((RING,)), DMA((RING,)), DMA((RING,)),
+            DMA, DMA, DMA, DMA, DMA, DMA,
             DMA, DMA,
-            DMA((RING,)), DMA((RING,)), DMA((RING,)), DMA((RING,)),
+            DMA, DMA, DMA, DMA,
             DMA, DMA,
         ],
         compiler_params=pltpu.CompilerParams(
             collective_id=1, has_side_effects=True, vmem_limit_bytes=VMEM_LIMIT
         ),
-    )(hn, weight, names, meta)
+    )(hn, weight, numbers)
 
 
 def per_device(
@@ -699,36 +731,19 @@
     labels,
     label_lengths,
 ):
-    section = lax.axis_index("section")
     micro = frames.shape[0]
-    mine, which = section // 2, lax.rem(section, 2)
-    block = lax.dynamic_index_in_dim(frames.reshape(micro, TOK, D), mine, 0, keepdims=False)
-    routes = routing[0, :, :, :, 0].reshape(micro, TOK)
-    same = routes[:, :, None] == routes[:, None, :]
-    earlier = jnp.arange(TOK)[:, None] < jnp.arange(TOK)[None, :]
-    rank = jnp.sum((same & earlier[None]).astype(jnp.int32), axis=1)
-    spots = (8 * routes + rank).astype(F32)
-    spots = jnp.pad(spots, ((0, 0), (0, D - TOK)), constant_values=-1.0)
-    aux = jnp.concatenate([norm_gain, spots, jnp.zeros((3, D), F32)], axis=0)
-    hn = run_moe(block, w_in[0, 0], w_out[0, 0], router[0].T, aux, head_gain.reshape(1, D))
-
-    count = labels.shape[2]
-    own = lax.dynamic_index_in_dim(labels.reshape(-1, count), section, 0, keepdims=False)
-    span = lax.dynamic_index_in_dim(frame_lengths.reshape(-1), section, 0, keepdims=False)
-    length = lax.dynamic_index_in_dim(label_lengths.reshape(-1), section, 0, keepdims=False)
-    names = jnp.concatenate([own, jnp.zeros((1,), jnp.int32), jnp.full((115,), -2, jnp.int32)]).astype(F32)
-    names = jnp.broadcast_to(names[None], (8, 128))
-    ext = jnp.concatenate([jnp.stack([jnp.zeros_like(own), own], axis=1).reshape(-1), jnp.zeros((1,), jnp.int32)])
-    skip = jnp.concatenate([jnp.zeros((2,), bool), (ext[2:] != 0) & (ext[2:] != ext[:-2])])
-    skip = jnp.pad(skip.astype(F32), (0, 128 - skip.shape[0]))
-    skip_back = jnp.concatenate([skip[2:], jnp.zeros((2,), F32)])
-    meta = jnp.stack(
-        [jnp.full((128,), span).astype(F32), jnp.full((128,), 2 * length).astype(F32), skip, skip_back]
-        + [jnp.zeros((128,), F32)] * 4
+    routes = routing[0, :, :, :, 0].reshape(micro, TOK).astype(F32)
+    routes = jnp.pad(routes, ((0, 8 - micro), (0, 128 - TOK)), constant_values=-1.0)
+    hn = run_moe(
+        frames.reshape(micro, TOK, D), w_in[0, 0], w_out[0, 0], router[0].T, norm_gain, routes, head_gain.reshape(1, D)
     )
-    weight = jnp.pad(head_weight, ((0, 0), (0, WIDE - head_weight.shape[1])))
-    losses, grad = run_head(hn, weight, names, meta)
-    return losses[0:1, 0:1], grad[: head_weight.shape[1]].T
+    pairs, count = 2 * micro, labels.shape[2]
+    numbers = jnp.concatenate(
+        [labels.reshape(pairs, count), frame_lengths.reshape(pairs, 1), label_lengths.reshape(pairs, 1)], axis=1
+    )
+    numbers = jnp.pad(numbers.astype(F32), ((0, 0), (0, 128 - numbers.shape[1])))
+    losses, grad = run_head(hn, head_weight, numbers)
+    return losses[0:1, 0:1], grad
 
 
 def solution(mesh):

time: 387 us -> 297 us (0.77)
  Pallas kernels: 366 us -> 285 us
  local copies, waits for them, and re-layouts: 15.4 us -> 9.52 us
    pallas_call x1, Pallas kernels: 257 us -> 188 us  [run_moe(): pl.pallas_call(moe_kernel, out_shape=jax.ShapeDtypeStruct((2, FRAMES, HAL...]
    pallas_call x1, Pallas kernels: 109 us -> 96.7 us  [run_head(): pl.pallas_call(head_kernel, out_shape=(jax.ShapeDtypeStruct((8, 128), F32...]
where the time goes in v2:
time: 297 us
  Pallas kernels  285 us (96%)
  local copies, waits for them, and re-layouts  9.52 us (3%)
    pallas_call x1, Pallas kernels, run_moe(): pl.pallas_call(moe_kernel, out_shape=jax.ShapeDtypeStruct((2, FRAMES, HAL...  188 us
    pallas_call x1, Pallas kernels, run_head(): pl.pallas_call(head_kernel, out_shape=(jax.ShapeDtypeStruct((8, 128), F32...  96.7 us

profile of v2, /device:TPU:1, one launch (start us, length us, event | category | flops | bytes accessed | tf_op | source)
XLA Modules:
  0.0 296.8 jit_solution(9723822553063430527)
XLA Ops:
  0.6 0.0 copy-start
  0.6 0.9 copy.19
  1.5 0.1 reshape.25
  1.6 0.8 copy.20
  2.4 0.1 reshape.26
  2.4 0.8 add_convert_fusion
  3.2 0.6 pad.9.numbers
  3.8 0.7 convert_reduce_fusion
  4.5 0.1 convert_element_type.12
  4.6 0.6 pad.8.routes
  5.2 1.3 reshape.21.head_gain
  6.5 188.5 %shard_map.122.hn = bf16[2,48,640]{2,1,0:T(8,128)(2,1)} custom-call(bf16[4,96,1280]{2,1,0:T(8,128)(2,1)} %bitcast.7, bf16[1280,256]{1,0:T(8,128)(2,1)} %bitcast.8, bf16[256,1280]{1,0:T(8,128)(2,1)} %bitcast.9, bf16[16,1280]{1,0:T(8,128)(2,1)} %bitcast.10, f32[1,1280]{1,0:T(1,128)} %gain.1, f32[8,128]{1,0:T(8,128)} %pad.8.routes, f32[1,1280]{1,0:T(1,128)} %reshape.21.head_gain), custom_call_target="tpu_custom_call" | custom-call | tf_op jit(solution)/shard_map/pallas_call | solution.py:359
  195.0 0.0 copy-done
  195.0 1.5 copy.23.weight
  196.5 96.7 %shard_map.123 = (f32[8,128]{1,0:T(8,128)}, bf16[1280,500]{1,0:T(8,128)(2,1)}) custom-call(bf16[2,48,640]{2,1,0:T(8,128)(2,1)} %shard_map.122.hn, bf16[1280,500]{1,0:T(8,128)(2,1)} %copy.23.weight, f32[8,128]{1,0:T(8,128)} %pad.9.numbers), custom_call_target="tpu_custom_call" | custom-call | tf_op jit(solution)/shard_map/pallas_call | solution.py:684
  293.2 1.2 slice.3
  294.4 2.5 copy.24
Async XLA Ops:
  0.6 194.3 %copy-start = (bf16[1280,500]{0,1:T(8,128)(2,1)S(1)}, bf16[1280,500]{0,1:T(8,128)(2,1)}, u32[]{:S(2)}) copy-start(bf16[1280,500]{0,1:T(8,128)(2,1)} %param.18) | copy-start | bytes 3840004

commit v3 on v2

--- a/solution.py
+++ b/solution.py
@@ -13,7 +13,7 @@
 F32, BF16 = jnp.float32, jnp.bfloat16
 D, HALF, EFF, LAYERS, RING, TOK, FRAMES = 1280, 640, 256, 8, 16, 96, 48
 PIECES = 16
-SKEW = 3
+SKEW = 4
 TURNS = PIECES // 4
 CHUNKS = LAYERS * PIECES
 IN_ROWS, OUT_ROWS = D // PIECES, EFF // PIECES
@@ -23,6 +23,8 @@
 VMEM = pltpu.VMEM
 DMA = pltpu.SemaphoreType.DMA
 VMEM_LIMIT = 56 * 1024 * 1024
+PLANE = sorted([(a, b) for a in range(4) for b in range(4) if a or b], key=lambda d: -sum(min(v, 4 - v) for v in d))
+AROUND = sorted(range(1, RING), key=lambda d: -min(d, RING - d))
 
 
 def coords():
@@ -69,9 +71,12 @@
         pl.semaphore_signal(barrier, inc=1, device_id=(p // 4, z, lax.rem(p, 4)), device_id_type=MESH)
 
     loop(1, 32, greet)
-    pl.semaphore_signal(barrier, inc=1, device_id=(s, above, y), device_id_type=MESH)
-    pl.semaphore_signal(barrier, inc=1, device_id=(s, below, y), device_id_type=MESH)
-    pl.semaphore_wait(barrier, 33)
+
+    def greet_ring(i):
+        pl.semaphore_signal(barrier, inc=1, device_id=(s, lax.rem(z + i, RING), y), device_id_type=MESH)
+
+    loop(1, RING, greet_ring)
+    pl.semaphore_wait(barrier, 46)
 
     def in_rows(j):
         return pl.ds(pl.multiple_of(j * IN_ROWS, 16), IN_ROWS)
@@ -354,40 +359,6 @@
         each(small(lax.rem(x + gap, 4)), sent)
 
 
-def run_moe(frames, w_in, w_out, router, gain, routes, head_gain):
-    anywhere, local = pl.BlockSpec(memory_space=pl.ANY), pl.BlockSpec(memory_space=VMEM)
-    return pl.pallas_call(
-        moe_kernel,
-        out_shape=jax.ShapeDtypeStruct((2, FRAMES, HALF), BF16),
-        in_specs=[anywhere, anywhere, anywhere, local, local, local, local],
-        out_specs=local,
-        scratch_shapes=[
-            VMEM((LAYERS, D, EFF), BF16),
-            VMEM((LAYERS, EFF, D), BF16),
-            VMEM((8, D), F32),
-            VMEM((LAYERS, 16, D), BF16),
-            VMEM((LAYERS, 8, D), F32),
-            VMEM((TOK, D), BF16),
-            VMEM((RING, 16, HALF), BF16),
-            VMEM((RING, 16, HALF), BF16),
-            VMEM((RING, 16, HALF), BF16),
-            VMEM((RING, 16, HALF), BF16),
-            VMEM((TURNS, IN_ROWS, EFF), BF16),
-            VMEM((TURNS, OUT_ROWS, D), BF16),
-            VMEM((2, FRAMES, HALF), BF16),
-            VMEM((2, FRAMES, HALF), BF16),
-            DMA((CHUNKS,)), DMA((CHUNKS,)), DMA, DMA,
-            DMA((LAYERS,)), DMA((LAYERS,)), DMA((LAYERS,)), DMA((LAYERS,)),
-            DMA((4, TURNS)), DMA((2, TURNS)), DMA((2, TURNS)), DMA((2, 4)), DMA((2, LAYERS)),
-            DMA, DMA, DMA, DMA,
-            DMA, DMA, DMA,
-        ],
-        compiler_params=pltpu.CompilerParams(
-            collective_id=0, has_side_effects=True, vmem_limit_bytes=VMEM_LIMIT
-        ),
-    )(frames, w_in, w_out, router, gain, routes, head_gain)
-
-
 def flip(block):
     rows = block.shape[0]
     if rows < 128:
@@ -410,7 +381,7 @@
 
 
 def head_kernel(
-    hn, weight, numbers, loss_out, grad_out,
+    fetch, hn, weight, numbers, loss_out, grad_out,
     rows_all, names, names_all, logits, stats, stats_all, emit, ahead, behind, notes, notes_all, grads, partial,
     half_out, half_in, pieces, pieces_all, total, totals,
     up_send, up_got, down_send, down_got, name_send, name_got, stat_send, stat_got, note_send, note_got,
@@ -420,26 +391,17 @@
     me = 4 * x + y
     pair = (s + 1 - 2 * c, z, y)
     above, below = lax.rem(z + 1, RING), lax.rem(z + RING - 1, RING)
-    barrier = pltpu.get_barrier_semaphore()
 
     def chip(p):
         return (2 * (p // 4) + c, z, lax.rem(p, 4))
 
-    def greet(i):
-        pl.semaphore_signal(barrier, inc=1, device_id=(s, lax.rem(z + i, RING), y), device_id_type=MESH)
-        pl.semaphore_signal(barrier, inc=1, device_id=chip(lax.rem(me + i, RING)), device_id_type=MESH)
-
-    loop(1, RING, greet)
-    pl.semaphore_signal(barrier, inc=1, device_id=pair, device_id_type=MESH)
-    pl.semaphore_wait(barrier, 31)
-
     def along(act):
-        for i in range(1, RING):
+        for i in AROUND:
             act(lax.rem(z + i, RING))
 
     def across(act):
-        for i in range(1, RING):
-            act(lax.rem(me + i, RING))
+        for a, b in PLANE:
+            act(4 * lax.rem(x + a, 4) + lax.rem(y + b, 4))
 
     def rise(i, h):
         block = rows_all.at[lax.rem(z + RING - i, RING), h]
@@ -476,6 +438,7 @@
         return remote(names, names_all.at[z], name_send, name_got, (s, p, y))
 
     along(lambda p: name_to(p).start())
+    fetch.wait()
     names_all[z] = names[...]
     logits[:, WIDE - 128 : WIDE] = jnp.zeros((RING * FRAMES, 128), F32)
 
@@ -648,19 +611,24 @@
     all_but_one(pieces_all, piece_got)
     total[...] = sum(pieces_all[k].astype(F32) for k in range(RING)).astype(BF16)
 
-    def total_to(p):
-        return remote(total, totals.at[c, me], total_send, total_got, chip(p))
-
-    across(lambda p: total_to(p).start())
+    def pass_on(p):
+        return remote(totals.at[c, p], totals.at[c, p], last_send, last_got, pair)
+
+    for n, (a, b) in enumerate(PLANE):
+        p = 4 * lax.rem(x + a, 4) + lax.rem(y + b, 4)
+        remote(total, totals.at[c, me], total_send, total_got.at[n // 5], chip(p)).start()
     totals[c, me] = total[...]
-    all_but_one(totals.at[c], total_got)
-    last_swap = remote(totals.at[c], totals.at[c], last_send, last_got, pair)
-    last_swap.start()
-    remote(totals.at[1 - c], totals.at[1 - c], last_send, last_got, pair).wait_recv()
+    pass_on(me).start()
+    for g in range(3):
+        five = pieces.at[pl.ds(0, 5)]
+        pltpu.make_async_copy(five, five, total_got.at[g]).wait()
+        for a, b in PLANE[5 * g : 5 * g + 5]:
+            pass_on(4 * lax.rem(x + 4 - a, 4) + lax.rem(y + 4 - b, 4)).start()
+    pltpu.make_async_copy(totals.at[1 - c], totals.at[1 - c], last_got).wait()
     grad_out[:, 0:256] = totals[0].reshape(D, 256)
     grad_out[:, 256:SHARD] = totals[1].reshape(D, 256)[:, : SHARD - 256]
 
-    last_swap.wait_send()
+    pltpu.make_async_copy(totals.at[c], totals.at[c], last_send).wait()
     swap.wait_send()
     all_but_one(names_all, name_send)
     all_but_one(stats, stat_send)
@@ -679,43 +647,77 @@
     loop(0, 8, ring_sent)
 
 
-def run_head(hn, weight, numbers):
-    local = pl.BlockSpec(memory_space=VMEM)
+MOE_SCRATCH = [
+    VMEM((LAYERS, D, EFF), BF16),
+    VMEM((LAYERS, EFF, D), BF16),
+    VMEM((8, D), F32),
+    VMEM((LAYERS, 16, D), BF16),
+    VMEM((LAYERS, 8, D), F32),
+    VMEM((TOK, D), BF16),
+    VMEM((RING, 16, HALF), BF16),
+    VMEM((RING, 16, HALF), BF16),
+    VMEM((RING, 16, HALF), BF16),
+    VMEM((RING, 16, HALF), BF16),
+    VMEM((TURNS, IN_ROWS, EFF), BF16),
+    VMEM((TURNS, OUT_ROWS, D), BF16),
+    VMEM((2, FRAMES, HALF), BF16),
+    VMEM((2, FRAMES, HALF), BF16),
+    DMA((CHUNKS,)), DMA((CHUNKS,)), DMA, DMA,
+    DMA((LAYERS,)), DMA((LAYERS,)), DMA((LAYERS,)), DMA((LAYERS,)),
+    DMA((4, TURNS)), DMA((2, TURNS)), DMA((2, TURNS)), DMA((2, 4)), DMA((2, LAYERS)),
+    DMA, DMA, DMA, DMA,
+    DMA, DMA, DMA,
+]
+HEAD_SCRATCH = [
+    VMEM((RING, 2, FRAMES, HALF), BF16),
+    VMEM((8, 128), F32),
+    VMEM((RING, 8, 128), F32),
+    VMEM((RING * FRAMES, WIDE), F32),
+    VMEM((RING, 8, 128), F32),
+    VMEM((RING, 8, 128), F32),
+    VMEM((FRAMES, 128), F32),
+    VMEM((FRAMES, 128), F32),
+    VMEM((FRAMES, 128), F32),
+    VMEM((8, 128), F32),
+    VMEM((RING, 8, 128), F32),
+    VMEM((RING * FRAMES, WIDE), BF16),
+    VMEM((D, WIDE), F32),
+    VMEM((D, 256), BF16),
+    VMEM((D, 256), BF16),
+    VMEM((RING, PART, 256), BF16),
+    VMEM((RING, PART, 256), BF16),
+    VMEM((PART, 256), BF16),
+    VMEM((2, RING, PART, 256), BF16),
+    DMA((8, 2)), DMA((8, 2)), DMA((8, 2)), DMA((8, 2)),
+    DMA, DMA, DMA, DMA, DMA, DMA,
+    DMA, DMA,
+    DMA, DMA, DMA, DMA((3,)),
+    DMA, DMA,
+]
+
+
+def whole_kernel(
+    frames, w_in, w_out, router, gain, routes, head_gain, head_weight, numbers, loss_out, grad_out,
+    hn, weight, weight_got, *scratch,
+):
+    fetch = pltpu.make_async_copy(head_weight, weight, weight_got)
+    fetch.start()
+    moe_kernel(frames, w_in, w_out, router, gain, routes, head_gain, hn, *scratch[: len(MOE_SCRATCH)])
+    head_kernel(fetch, hn, weight, numbers, loss_out, grad_out, *scratch[len(MOE_SCRATCH) :])
+
+
+def run(*arrays):
+    anywhere, local = pl.BlockSpec(memory_space=pl.ANY), pl.BlockSpec(memory_space=VMEM)
     return pl.pallas_call(
-        head_kernel,
+        whole_kernel,
         out_shape=(jax.ShapeDtypeStruct((8, 128), F32), jax.ShapeDtypeStruct((D, SHARD), BF16)),
-        in_specs=[local] * 3,
+        in_specs=[anywhere] * 3 + [local] * 4 + [anywhere, local],
         out_specs=(local, local),
-        scratch_shapes=[
-            VMEM((RING, 2, FRAMES, HALF), BF16),
-            VMEM((8, 128), F32),
-            VMEM((RING, 8, 128), F32),
-            VMEM((RING * FRAMES, WIDE), F32),
-            VMEM((RING, 8, 128), F32),
-            VMEM((RING, 8, 128), F32),
-            VMEM((FRAMES, 128), F32),
-            VMEM((FRAMES, 128), F32),
-            VMEM((FRAMES, 128), F32),
-            VMEM((8, 128), F32),
-            VMEM((RING, 8, 128), F32),
-            VMEM((RING * FRAMES, WIDE), BF16),
-            VMEM((D, WIDE), F32),
-            VMEM((D, 256), BF16),
-            VMEM((D, 256), BF16),
-            VMEM((RING, PART, 256), BF16),
-            VMEM((RING, PART, 256), BF16),
-            VMEM((PART, 256), BF16),
-            VMEM((2, RING, PART, 256), BF16),
-            DMA((8, 2)), DMA((8, 2)), DMA((8, 2)), DMA((8, 2)),
-            DMA, DMA, DMA, DMA, DMA, DMA,
-            DMA, DMA,
-            DMA, DMA, DMA, DMA,
-            DMA, DMA,
-        ],
+        scratch_shapes=[VMEM((2, FRAMES, HALF), BF16), VMEM((D, SHARD), BF16), DMA] + MOE_SCRATCH + HEAD_SCRATCH,
         compiler_params=pltpu.CompilerParams(
-            collective_id=1, has_side_effects=True, vmem_limit_bytes=VMEM_LIMIT
+            collective_id=0, has_side_effects=True, vmem_limit_bytes=VMEM_LIMIT
         ),
-    )(hn, weight, numbers)
+    )(*arrays)
 
 
 def per_device(
@@ -734,15 +736,15 @@
     micro = frames.shape[0]
     routes = routing[0, :, :, :, 0].reshape(micro, TOK).astype(F32)
     routes = jnp.pad(routes, ((0, 8 - micro), (0, 128 - TOK)), constant_values=-1.0)
-    hn = run_moe(
-        frames.reshape(micro, TOK, D), w_in[0, 0], w_out[0, 0], router[0].T, norm_gain, routes, head_gain.reshape(1, D)
-    )
     pairs, count = 2 * micro, labels.shape[2]
     numbers = jnp.concatenate(
         [labels.reshape(pairs, count), frame_lengths.reshape(pairs, 1), label_lengths.reshape(pairs, 1)], axis=1
     )
     numbers = jnp.pad(numbers.astype(F32), ((0, 0), (0, 128 - numbers.shape[1])))
-    losses, grad = run_head(hn, head_weight, numbers)
+    losses, grad = run(
+        frames.reshape(micro, TOK, D), w_in[0, 0], w_out[0, 0], router[0].T, norm_gain, routes,
+        head_gain.reshape(1, D), head_weight, numbers,
+    )
     return losses[0:1, 0:1], grad
 
 

time: 297 us -> 286 us (0.963)
  Pallas kernels: 285 us -> 273 us
    pallas_call x2 -> x1, Pallas kernels: 285 us -> 273 us  [run(): pl.pallas_call(whole_kernel, out_shape=(jax.ShapeDtypeStruct((8, 128), F3...]
    unnamed x6 -> x4, local copies, waits for them, and re-layouts: 5.6 us -> 6.45 us
where the time goes in v3:
time: 286 us
  Pallas kernels  273 us (95%)
  local copies, waits for them, and re-layouts  10.4 us (4%)
    pallas_call x1, Pallas kernels, run(): pl.pallas_call(whole_kernel, out_shape=(jax.ShapeDtypeStruct((8, 128), F3...  273 us
    unnamed x4, local copies, waits for them, and re-layouts  6.45 us

profile of v3, /device:TPU:1, one launch (start us, length us, event | category | flops | bytes accessed | tf_op | source)
XLA Modules:
  0.0 285.8 jit_solution(15269623522198155390)
XLA Ops:
  0.6 0.8 copy.19
  1.4 0.1 reshape.25
  1.5 0.8 copy.20
  2.2 0.1 reshape.26
  2.3 0.8 add_convert_fusion
  3.1 0.6 pad.9.numbers
  3.7 0.7 convert_reduce_fusion
  4.4 0.1 convert_element_type.12
  4.5 0.6 pad.8.routes
  5.1 1.3 reshape.21.head_gain
  6.4 2.4 copy.23.head_weight
  8.8 273.3 %shard_map.122 = (f32[8,128]{1,0:T(8,128)}, bf16[1280,500]{1,0:T(8,128)(2,1)}) custom-call(bf16[4,96,1280]{2,1,0:T(8,128)(2,1)} %bitcast.7, bf16[1280,256]{1,0:T(8,128)(2,1)} %bitcast.8, bf16[256,1280]{1,0:T(8,128)(2,1)} %bitcast.9, bf16[16,1280]{1,0:T(8,128)(2,1)} %bitcast.10, f32[1,1280]{1,0:T(1,128)} %gain.1, f32[8,128]{1,0:T(8,128)} %pad.8.routes, ...), custom_call_target="tpu_custom_call" | custom-call | tf_op jit(solution)/shard_map/pallas_call | solution.py:711
  282.2 1.2 slice.3
  283.4 2.5 copy.24

commit v4 on v3

--- a/solution.py
+++ b/solution.py
@@ -18,7 +18,7 @@
 CHUNKS = LAYERS * PIECES
 IN_ROWS, OUT_ROWS = D // PIECES, EFF // PIECES
 SHARD, WIDE = 500, 512
-PART = D // RING
+PART = WIDE // 2 // RING
 HIGHEST = lax.Precision.HIGHEST
 VMEM = pltpu.VMEM
 DMA = pltpu.SemaphoreType.DMA
@@ -70,12 +70,14 @@
         p = lax.rem(4 * s + y + i, 32)
         pl.semaphore_signal(barrier, inc=1, device_id=(p // 4, z, lax.rem(p, 4)), device_id_type=MESH)
 
-    loop(1, 32, greet)
+    for i in range(1, 32):
+        greet(i)
 
     def greet_ring(i):
         pl.semaphore_signal(barrier, inc=1, device_id=(s, lax.rem(z + i, RING), y), device_id_type=MESH)
 
-    loop(1, RING, greet_ring)
+    for i in range(1, RING):
+        greet_ring(i)
     pl.semaphore_wait(barrier, 46)
 
     def in_rows(j):
@@ -382,7 +384,7 @@
 
 def head_kernel(
     fetch, hn, weight, numbers, loss_out, grad_out,
-    rows_all, names, names_all, logits, stats, stats_all, emit, ahead, behind, notes, notes_all, grads, partial,
+    rows_all, names, names_all, chosen_all, logits, stats, stats_all, emit, ahead, behind, notes, notes_all, grads, partial,
     half_out, half_in, pieces, pieces_all, total, totals,
     up_send, up_got, down_send, down_got, name_send, name_got, stat_send, stat_got, note_send, note_got,
     half_send, half_got, piece_send, piece_got, total_send, total_got, last_send, last_got,
@@ -471,14 +473,15 @@
         def side(h):
             return jnp.concatenate([rows_all[k, h] for k in blocks], axis=0)
 
-        value = dot(side(0), weight[0:HALF, :]) + dot(side(1), weight[HALF:D, :])
+        value = dot(side(0), weight[:, 0:HALF], ((1,), (1,))) + dot(side(1), weight[:, HALF:D], ((1,), (1,)))
         for n, k in enumerate(blocks):
             logits[frames_of(k), 0:SHARD] = value[n * FRAMES : (n + 1) * FRAMES]
         for k in blocks:
             block = logits[frames_of(k), :]
             peak = jnp.max(jnp.where(valid, block, -jnp.inf), axis=1, keepdims=True)
             weightsum = jnp.sum(jnp.where(valid, jnp.exp(block - peak), 0.0), axis=1, keepdims=True)
-            found = joined(dot(thirds(block), selector(k), ((1,), (1,))))
+            chosen_all[k] = selector(k)
+            found = joined(dot(thirds(block), chosen_all[k], ((1,), (1,))))
             stats[k] = pack(jnp.where(lane == 13, peak, jnp.where(lane == 14, weightsum, found)))
 
     def ring_step(i):
@@ -579,29 +582,29 @@
     along(lambda p: note_to(p).start())
     all_but_one(notes_all, note_got)
 
-    def spread(pair_at):
-        for k in (2 * pair_at, 2 * pair_at + 1):
+    def spread(group):
+        for k in [4 * group + n for n in range(4)]:
             packed = notes_all[k]
             known = flip(jnp.concatenate([packed, pltpu.roll(packed, 64, 1)], axis=0))[:FRAMES]
-            scattered = joined(dot(thirds(known), selector(k)))
+            scattered = joined(dot(thirds(known), chosen_all[k]))
             block = logits[frames_of(k), :]
             value = scattered - jnp.exp(block - known[:, 14:15]) * known[:, 13:14]
             grads[frames_of(k), :] = jnp.where(valid, value, 0.0).astype(BF16)
 
-    loop(0, RING // 2, spread)
+    loop(0, RING // 4, spread)
     for h in range(2):
-        partial[HALF * h : HALF * (h + 1), :] = dot(
-            rows_all[:, h].reshape(RING * FRAMES, HALF), grads[...], ((0,), (0,))
+        partial[:, HALF * h : HALF * (h + 1)] = dot(
+            grads[...], rows_all[:, h].reshape(RING * FRAMES, HALF), ((0,), (0,))
         )
 
     def mine(core):
         return pl.ds(pl.multiple_of(256 * core, 256), 256)
 
-    half_out[...] = partial[:, mine(1 - c)].astype(BF16)
+    half_out[...] = partial[mine(1 - c), :].astype(BF16)
     swap = remote(half_out, half_in, half_send, half_got, pair)
     swap.start()
     swap.wait_recv()
-    pieces[...] = (partial[:, mine(c)] + half_in[...].astype(F32)).astype(BF16).reshape(RING, PART, 256)
+    pieces[...] = (partial[mine(c), :] + half_in[...].astype(F32)).astype(BF16).reshape(RING, PART, D)
 
     def piece_to(p):
         return remote(pieces.at[p], pieces_all.at[me], piece_send, piece_got, chip(p))
@@ -625,8 +628,8 @@
         for a, b in PLANE[5 * g : 5 * g + 5]:
             pass_on(4 * lax.rem(x + 4 - a, 4) + lax.rem(y + 4 - b, 4)).start()
     pltpu.make_async_copy(totals.at[1 - c], totals.at[1 - c], last_got).wait()
-    grad_out[:, 0:256] = totals[0].reshape(D, 256)
-    grad_out[:, 256:SHARD] = totals[1].reshape(D, 256)[:, : SHARD - 256]
+    grad_out[0:256, :] = totals[0].reshape(256, D)
+    grad_out[256:SHARD, :] = totals[1].reshape(256, D)[: SHARD - 256, :]
 
     pltpu.make_async_copy(totals.at[c], totals.at[c], last_send).wait()
     swap.wait_send()
@@ -672,6 +675,7 @@
     VMEM((RING, 2, FRAMES, HALF), BF16),
     VMEM((8, 128), F32),
     VMEM((RING, 8, 128), F32),
+    VMEM((RING, 128, WIDE), BF16),
     VMEM((RING * FRAMES, WIDE), F32),
     VMEM((RING, 8, 128), F32),
     VMEM((RING, 8, 128), F32),
@@ -681,13 +685,13 @@
     VMEM((8, 128), F32),
     VMEM((RING, 8, 128), F32),
     VMEM((RING * FRAMES, WIDE), BF16),
-    VMEM((D, WIDE), F32),
-    VMEM((D, 256), BF16),
-    VMEM((D, 256), BF16),
-    VMEM((RING, PART, 256), BF16),
-    VMEM((RING, PART, 256), BF16),
-    VMEM((PART, 256), BF16),
-    VMEM((2, RING, PART, 256), BF16),
+    VMEM((WIDE, D), F32),
+    VMEM((256, D), BF16),
+    VMEM((256, D), BF16),
+    VMEM((RING, PART, D), BF16),
+    VMEM((RING, PART, D), BF16),
+    VMEM((PART, D), BF16),
+    VMEM((2, RING, PART, D), BF16),
     DMA((8, 2)), DMA((8, 2)), DMA((8, 2)), DMA((8, 2)),
     DMA, DMA, DMA, DMA, DMA, DMA,
     DMA, DMA,
@@ -710,10 +714,10 @@
     anywhere, local = pl.BlockSpec(memory_space=pl.ANY), pl.BlockSpec(memory_space=VMEM)
     return pl.pallas_call(
         whole_kernel,
-        out_shape=(jax.ShapeDtypeStruct((8, 128), F32), jax.ShapeDtypeStruct((D, SHARD), BF16)),
+        out_shape=(jax.ShapeDtypeStruct((8, 128), F32), jax.ShapeDtypeStruct((SHARD, D), BF16)),
         in_specs=[anywhere] * 3 + [local] * 4 + [anywhere, local],
         out_specs=(local, local),
-        scratch_shapes=[VMEM((2, FRAMES, HALF), BF16), VMEM((D, SHARD), BF16), DMA] + MOE_SCRATCH + HEAD_SCRATCH,
+        scratch_shapes=[VMEM((2, FRAMES, HALF), BF16), VMEM((SHARD, D), BF16), DMA] + MOE_SCRATCH + HEAD_SCRATCH,
         compiler_params=pltpu.CompilerParams(
             collective_id=0, has_side_effects=True, vmem_limit_bytes=VMEM_LIMIT
         ),
@@ -743,9 +747,9 @@
     numbers = jnp.pad(numbers.astype(F32), ((0, 0), (0, 128 - numbers.shape[1])))
     losses, grad = run(
         frames.reshape(micro, TOK, D), w_in[0, 0], w_out[0, 0], router[0].T, norm_gain, routes,
-        head_gain.reshape(1, D), head_weight, numbers,
+        head_gain.reshape(1, D), head_weight.T, numbers,
     )
-    return losses[0:1, 0:1], grad
+    return losses[0:1, 0:1], grad.T
 
 
 def solution(mesh):

time: 286 us -> 284 us (level)
    unnamed x4 -> x3, local copies, waits for them, and re-layouts: 6.45 us -> 3.97 us
where the time goes in v4:
time: 284 us; the launch traced here: 283 us
  Pallas kernels  273 us (96%)
  local copies, waits for them, and re-layouts  7.89 us (3%)
    pallas_call x1, Pallas kernels, run(): pl.pallas_call(whole_kernel, out_shape=(jax.ShapeDtypeStruct((8, 128), F3...  273 us

profile of v4, /device:TPU:1, one launch (start us, length us, event | category | flops | bytes accessed | tf_op | source)
XLA Modules:
  0.0 283.1 jit_solution(3628179316982857531)
XLA Ops:
  0.6 0.8 copy.17
  1.4 0.1 reshape.25
  1.5 0.8 copy.18
  2.2 0.1 reshape.26
  2.3 0.8 add_convert_fusion
  3.1 0.6 pad.9.numbers
  3.7 0.7 convert_reduce_fusion
  4.4 0.1 convert_element_type.12
  4.5 0.6 pad.8.routes
  5.1 1.3 reshape.21.head_gain
  6.4 273.1 %shard_map.122 = (f32[8,128]{1,0:T(8,128)}, bf16[500,1280]{1,0:T(8,128)(2,1)}) custom-call(bf16[4,96,1280]{2,1,0:T(8,128)(2,1)} %bitcast.11, bf16[1280,256]{1,0:T(8,128)(2,1)} %bitcast.12, bf16[256,1280]{1,0:T(8,128)(2,1)} %bitcast.13, bf16[16,1280]{1,0:T(8,128)(2,1)} %bitcast.14, f32[1,1280]{1,0:T(1,128)} %gain.1, f32[8,128]{1,0:T(8,128)} %pad.8.routes, ...), custom_call_target="tpu_custom_call" | custom-call | tf_op jit(solution)/shard_map/pallas_call | solution.py:715
  279.5 1.2 slice.3
  280.7 2.4 copy.22

commit v5 on v4

--- a/solution.py
+++ b/solution.py
@@ -334,7 +334,7 @@
             wait_all(answer, answer_send)
 
         loop(0, LAYERS, layer_step)
-        hn = rms(state[...].astype(F32), head_gain[...])
+        hn = rms(state[...].astype(F32), head_gain[...].reshape(1, D))
         for h in range(2):
             hn_out[h] = hn[:FRAMES, HALF * h : HALF * (h + 1)]
             passed[h] = hn[FRAMES:, HALF * h : HALF * (h + 1)]
@@ -564,7 +564,7 @@
     tail = jnp.where(ends, final, LOG_ZERO)
     top = jnp.max(tail, axis=1, keepdims=True)
     likely = top + jnp.log(jnp.sum(jnp.where(ends, jnp.exp(final - top), 0.0), axis=1, keepdims=True))
-    loss_out[...] = jnp.broadcast_to(-likely, (8, 128))
+    loss_out[...] = -likely
     when = lax.broadcasted_iota(jnp.int32, (FRAMES, 128), 0).astype(F32)
     occupied = jnp.where(
         (when < span) & (lane < 25), -jnp.exp(ahead[...] + behind[...] - likely), 0.0
@@ -714,7 +714,7 @@
     anywhere, local = pl.BlockSpec(memory_space=pl.ANY), pl.BlockSpec(memory_space=VMEM)
     return pl.pallas_call(
         whole_kernel,
-        out_shape=(jax.ShapeDtypeStruct((8, 128), F32), jax.ShapeDtypeStruct((SHARD, D), BF16)),
+        out_shape=(jax.ShapeDtypeStruct((1, 1), F32), jax.ShapeDtypeStruct((SHARD, D), BF16)),
         in_specs=[anywhere] * 3 + [local] * 4 + [anywhere, local],
         out_specs=(local, local),
         scratch_shapes=[VMEM((2, FRAMES, HALF), BF16), VMEM((SHARD, D), BF16), DMA] + MOE_SCRATCH + HEAD_SCRATCH,
@@ -747,9 +747,9 @@
     numbers = jnp.pad(numbers.astype(F32), ((0, 0), (0, 128 - numbers.shape[1])))
     losses, grad = run(
         frames.reshape(micro, TOK, D), w_in[0, 0], w_out[0, 0], router[0].T, norm_gain, routes,
-        head_gain.reshape(1, D), head_weight.T, numbers,
+        head_gain, head_weight.T, numbers,
     )
-    return losses[0:1, 0:1], grad.T
+    return losses, grad.T
 
 
 def solution(mesh):

time: 284 us -> 283 us (level)
  no operation moved by 1% of the time
where the time goes in v5:
time: 283 us; the launch traced here: 282 us
  Pallas kernels  273 us (96%)
  local copies, waits for them, and re-layouts  5.41 us (2%)
    pallas_call x1, Pallas kernels, run(): pl.pallas_call(whole_kernel, out_shape=(jax.ShapeDtypeStruct((1, 1), F32)...  273 us

profile of v5, /device:TPU:1, one launch (start us, length us, event | category | flops | bytes accessed | tf_op | source)
XLA Modules:
  0.0 282.4 jit_solution(9138642116621518647)
XLA Ops:
  0.6 0.8 copy.17
  1.4 0.1 reshape.21
  1.5 0.8 copy.18
  2.2 0.1 reshape.22
  2.3 0.8 add_convert_fusion
  3.1 0.6 pad.9.numbers
  3.7 0.7 convert_reduce_fusion
  4.4 0.1 convert_element_type.12
  4.5 0.6 pad.8.routes
  5.1 273.1 %shard_map.122 = (f32[1,1]{1,0:T(1,128)}, bf16[500,1280]{1,0:T(8,128)(2,1)}) custom-call(bf16[4,96,1280]{2,1,0:T(8,128)(2,1)} %bitcast.11, bf16[1280,256]{1,0:T(8,128)(2,1)} %bitcast.12, bf16[256,1280]{1,0:T(8,128)(2,1)} %bitcast.13, bf16[16,1280]{1,0:T(8,128)(2,1)} %bitcast.14, f32[1,1280]{1,0:T(1,128)} %gain.1, f32[8,128]{1,0:T(8,128)} %pad.8.routes, ...), custom_call_target="tpu_custom_call" | custom-call | tf_op jit(solution)/shard_map/pallas_call | solution.py:715
  278.8 2.4 copy.24
